TPU v7x, 512 devices: a whole 4x4x16 slice. The times are simulated.
512 devices in a mesh: grp: 8 (over x_lo, y), slab: 64 (over z, x_hi, core).
Axes of the slice: x: 4 (x_hi: 2, x_lo: 2; x = x_hi * 2 + x_lo), y: 4, z: 16, core: 2. Of those that a mesh axis runs over, the one named last changes fastest.
Arguments:
- velocity: float32 [64, 512, 512], P('grp', 'slab'), may hold values from -6 to 6
- rate: float32 [64, 512, 512], P('grp', 'slab'), may hold values from 0.02 to 0.16
- forcing: float32 [64, 512, 512], P('grp', 'slab'), may hold values from -3 to 3
- anchor_line: int32 [8192], P(('grp', 'slab')), may hold values from 0 to 63
- anchor_z: int32 [8192], P(('grp', 'slab')), may hold values from 0 to 384
- assign: int32 [8192, 1], P(('grp', 'slab')), may hold values from 0 to 63; in each aligned block of 16 rows (0 to 15, 16 to 31, ...) at most 2 rows name the same one
- spectral: float32 [2048, 64], replicated, may hold values from -0.75 to 0.75
- dense: float32 [68, 64], replicated, may hold values from -4 to 4
- momentum: float32 [2048, 64], P(('grp', 'slab')), may hold values from -0.3125 to 0.3125
Outputs:
- field_out: float32 [64, 512, 512], P('grp', 'slab')
- trainer_loss: float32 [8, 64], P('grp', 'slab')
- spectral_new: float32 [2048, 64], replicated
- dense_new: float32 [68, 64], replicated
- momentum_new: float32 [2048, 64], P(('grp', 'slab'))
Inputs may be any that keep to these rules, and one draw needn't show every extreme that they name: `assign`: within the 16 lines of one device no trainer is named more than 2 times, and in some device's lines one trainer is named exactly 2 times.
All inputs are finite; a program needn't handle non-finite values.
Results may differ from a plain program's by a relative error of at most 0.0001.
Values sent between devices are 32-bit elements; how exact they have to be, the bound alone decides.
A program may use at most 64 MiB of HBM per device.

v0:
```python
import jax
import jax.numpy as jnp
from jax import lax
from jax.sharding import PartitionSpec as P

STEPS = 2
SUB = 128
MODES = 16


decay_rate = 0.9
learn_rate = 0.5
dense_rate = 3.0


def extended(cells, sides, width):
    for axis, dim in sides:
        count = lax.axis_size(axis)
        ends = count - 1
        head = lax.slice_in_dim(cells, 0, width, axis=dim)
        tail = lax.slice_in_dim(cells, cells.shape[dim] - width, cells.shape[dim], axis=dim)
        cells = jnp.concatenate(
            [
                lax.ppermute(tail, axis, [(i, (i + 1) % count) for i in range(ends)]),
                cells,
                lax.ppermute(head, axis, [((i + 1) % count, i) for i in range(ends)]),
            ],
            axis=dim,
        )
    return cells


def tables():
    counts = jnp.arange(SUB, dtype=jnp.int32)
    waves = jnp.arange(MODES, dtype=jnp.int32)
    phase = counts[:, None] * waves[None, :] % SUB
    angle = phase.astype(jnp.float32) * (2.0 * jnp.pi / SUB)
    weight_k = jnp.where(waves == 0, 1.0, 2.0).astype(jnp.float32) / SUB
    return (jnp.cos(angle), jnp.sin(angle), weight_k)


def line_errors(spectral, dense, inputs, targets, valid):
    highest = lax.Precision.HIGHEST
    width = dense.shape[1]
    mixing = dense[:width]
    lift_gain, lift_bias, layer_bias, projection = (
        dense[width],
        dense[width + 1],
        dense[width + 2],
        dense[width + 3],
    )
    cosine, sine, weight_k = tables()
    hidden = inputs[:, None, :] * lift_gain[None, :, None] + lift_bias[None, :, None]
    real_in = jnp.einsum("bws,sk->bwk", hidden, cosine, precision=highest)
    imag_in = -jnp.einsum("bws,sk->bwk", hidden, sine, precision=highest)
    blocks = spectral.reshape(2, MODES, width, width)
    w_real, w_imag = (blocks[0], blocks[1])
    real_out = jnp.einsum("bwk,kwv->bvk", real_in, w_real, precision=highest) - jnp.einsum(
        "bwk,kwv->bvk", imag_in, w_imag, precision=highest
    )
    imag_out = jnp.einsum("bwk,kwv->bvk", real_in, w_imag, precision=highest) + jnp.einsum(
        "bwk,kwv->bvk", imag_in, w_real, precision=highest
    )
    spatial = jnp.einsum(
        "bvk,sk->bvs", real_out * weight_k, cosine, precision=highest
    ) - jnp.einsum("bvk,sk->bvs", imag_out * weight_k, sine, precision=highest)
    before = (
        spatial
        + jnp.einsum("bws,wv->bvs", hidden, mixing, precision=highest)
        + layer_bias[None, :, None]
    )
    after = jax.nn.gelu(before)
    output = jnp.einsum("bvs,v->bs", after, projection, precision=highest)
    return jnp.sum((output - targets) ** 2, axis=1) * valid


def gradients_of(spectral, dense, inputs, targets, valid, scale):

    def loss_fn(spec, dens):
        errors = line_errors(spec, dens, inputs, targets, valid)
        return (jnp.sum(errors) * scale, errors)

    value, pullback, errors = jax.vjp(loss_fn, spectral, dense, has_aux=True)
    grad_spec, grad_dense = pullback(jnp.ones((), jnp.float32))
    return (grad_spec, grad_dense, errors)


def local(velocity, rate, forcing, anchor_line, anchor_z, assign, spectral, dense, momentum):
    field_now = velocity
    previous = velocity
    change = velocity
    for number in range(STEPS):
        previous = field_now
        padded = extended(field_now, (("grp", 0), ("slab", 1)), 1)
        beside = padded[2:, 1:-1] + padded[:-2, 1:-1] + padded[1:-1, 2:] + padded[1:-1, :-2]
        beside = beside + jnp.roll(field_now, 1, 2) + jnp.roll(field_now, -1, 2)
        change = rate * (beside - 6.0 * field_now) + forcing
        field_now = field_now + change
    cells_x, cells_y, cells_z = velocity.shape
    line_count = anchor_line.shape[0]
    windows = jax.vmap(lambda row, start: lax.dynamic_slice_in_dim(row, start, SUB))
    inputs = windows(
        jnp.take(previous.reshape(cells_x * cells_y, cells_z), anchor_line, axis=0), anchor_z
    )
    targets = windows(
        jnp.take(change.reshape(cells_x * cells_y, cells_z), anchor_line, axis=0), anchor_z
    )
    n_slab = lax.axis_size("slab")
    devices = lax.axis_size("grp") * n_slab
    scale = 1.0 / (devices * line_count * SUB)
    dest = assign[:, 0]
    onehot = (dest[:, None] == jnp.arange(n_slab, dtype=jnp.int32)[None, :]).astype(jnp.int32)
    grad_spec, grad_dense, errors = gradients_of(
        spectral, dense, inputs, targets, jnp.ones((line_count,), jnp.float32), scale
    )
    partial_loss = jnp.dot(errors, onehot.astype(jnp.float32), precision=lax.Precision.HIGHEST) / (
        line_count * SUB
    )
    trainer_loss = lax.psum_scatter(partial_loss, "slab", scatter_dimension=0, tiled=True).reshape(
        1, 1
    )
    grad_rows = lax.psum_scatter(grad_spec, ("grp", "slab"), scatter_dimension=0, tiled=True)
    grad_dense = lax.psum(grad_dense, ("grp", "slab"))
    piece_rows = grad_rows.shape[0]
    position = lax.axis_index(("grp", "slab"))
    own_rows = lax.dynamic_slice_in_dim(spectral, position * piece_rows, piece_rows, 0)
    momentum_new = decay_rate * momentum + grad_rows
    updated_rows = own_rows - learn_rate * momentum_new
    spectral_new = lax.all_gather(updated_rows, ("grp", "slab"), axis=0, tiled=True)
    dense_new = dense - dense_rate * grad_dense
    return (field_now, trainer_loss, spectral_new, dense_new, momentum_new)


def solution(mesh):
    placed = (
        P("grp", "slab", None),
        P("grp", "slab", None),
        P("grp", "slab", None),
        P(("grp", "slab")),
        P(("grp", "slab")),
        P(("grp", "slab"), None),
        P(),
        P(),
        P(("grp", "slab"), None),
    )
    return jax.shard_map(
        local,
        mesh=mesh,
        in_specs=placed,
        out_specs=(P("grp", "slab", None), P("grp", "slab"), P(), P(), P(("grp", "slab"), None)),
        check_vma=False,
    )
```

profile of v0, /device:TPU:1, one launch (start us, length us, event | category | flops | bytes accessed | tf_op | source)
XLA Modules:
  0.0 1307.5 jit_solution(13994378432444662468)
XLA Ops:
  8.0 1.3 collective-permute-start
  9.3 4.7 collective-permute-start.1
  17.4 8.7 collective-permute-start.2
  26.1 1.9 collective-permute-start.3
  28.1 1.3 dynamic-slice.6
  30.7 2.0 collective-permute-start.5
  32.7 1.3 collective-permute-start.4
  34.1 3.1 collective-permute-done.4
  37.2 3.8 collective-permute-start.6
  41.1 3.6 collective-permute-start.7
  47.0 32.3 %while.2 = (s32[]{:T(128)}, f32[16,512]{1,0:T(8,128)S(1)}, s32[16,2]{0,1:T(2,128)S(1)}, f32[16,128]{1,0:T(8,128)S(1)}, s32[]{:T(128)}, /*index=5*/s32[]{:T(128)}) while((s32[]{:T(128)}, f32[16,512]{1,0:T(8,128)S(1)}, s32[16,2]{0,1:T(2,128)S(1)}, f32[16,128]{1,0:T(8,128)S(1)}, s32[]{:T(128)}, /*index=5*/s32[]{:T(128)}) %tuple.60), condition=%wide.while_cond, body=%wide.while_body.sunk | while | flops 2 | bytes 2169 | solution.py:101
  47.6 1.3 dynamic-slice.18
  49.6 1.3 dynamic-slice.18
  51.6 1.3 dynamic-slice.18
  53.7 1.3 dynamic-slice.18
  55.7 1.3 dynamic-slice.18
  57.7 1.3 dynamic-slice.18
  59.7 1.3 dynamic-slice.18
  61.7 1.3 dynamic-slice.18
  63.8 1.3 dynamic-slice.18
  65.8 1.3 dynamic-slice.18
  67.8 1.3 dynamic-slice.18
  69.8 1.3 dynamic-slice.18
  71.8 1.3 dynamic-slice.18
  73.9 1.3 dynamic-slice.18
  75.9 1.3 dynamic-slice.18
  77.9 1.3 dynamic-slice.18
  79.3 1.4 convolution_negate_fusion
  80.7 1.4 fusion.38
  82.8 32.1 %while.3 = (s32[]{:T(128)}, f32[16,512]{1,0:T(8,128)S(1)}, s32[16,2]{0,1:T(2,128)S(1)}, f32[16,128]{1,0:T(8,128)S(1)}, s32[]{:T(128)}, /*index=5*/s32[]{:T(128)}) while((s32[]{:T(128)}, f32[16,512]{1,0:T(8,128)S(1)}, s32[16,2]{0,1:T(2,128)S(1)}, f32[16,128]{1,0:T(8,128)S(1)}, s32[]{:T(128)}, /*index=5*/s32[]{:T(128)}) %tuple.68), condition=%wide.while_cond.1, body=%wide.while_body.1.sunk | while | flops 2 | bytes 2169 | solution.py:101
  83.4 1.4 dynamic-slice.20
  85.4 1.4 dynamic-slice.20
  87.4 1.4 dynamic-slice.20
  89.4 1.4 dynamic-slice.20
  91.4 1.4 dynamic-slice.20
  93.4 1.4 dynamic-slice.20
  95.4 1.4 dynamic-slice.20
  97.4 1.4 dynamic-slice.20
  99.4 1.4 dynamic-slice.20
  101.4 1.4 dynamic-slice.20
  103.4 1.4 dynamic-slice.20
  105.4 1.4 dynamic-slice.20
  107.4 1.4 dynamic-slice.20
  109.4 1.4 dynamic-slice.20
  111.4 1.4 dynamic-slice.20
  113.3 1.4 dynamic-slice.20
  117.3 1.0 fusion.72
  118.3 1.0 fusion.35
  122.8 1.3 fusion.6
  124.2 1.4 fusion.186
  127.4 1.0 fusion.82
  130.2 1.1 fusion.4
  132.3 1.0 convolution_add_fusion.1
  133.3 1.1 fusion.171
  134.6 1.0 fusion
  135.6 1.0 fusion.1
  136.7 1.1 pad_add_fusion
  138.8 135.1 %all-reduce.7 = f32[64]{0:T(128)S(1)} all-reduce(f32[64]{0:T(128)S(1)} %fusion.11), channel_id=2, replica_groups=mesh['grp'=8,'slab'=64] {'slab'}, use_global_device_ids=true, to_apply=%region_1.3.clone | all-reduce | flops 64 | bytes 512
  273.9 1.2 dynamic-slice.7
  275.2 110.7 %psum.7 = f32[68,64]{0,1:T(8,128)S(1)} all-reduce(f32[68,64]{0,1:T(8,128)S(1)} %pad_add_fusion.1), channel_id=1, replica_groups=mesh['grp'=8,'slab'=64] {'grp','slab'}, use_global_device_ids=true, to_apply=%region_6.8 | all-reduce | flops 4352 | bytes 34816 | tf_op jit(solution)/shard_map/psum | solution.py:123
  386.5 229.7 %all-reduce.11.cloned.1.call-done = f32[2048,64]{1,0:T(8,128)} async-done(((f32[2048,64]{1,0:T(8,128)}), f32[2048,64]{1,0:T(8,128)}) %all-reduce.11.cloned.1.call-update) | async-done | bytes 524304
  616.2 1.3 subtract_bitcast_fusion
  617.5 682.0 %all-gather = f32[512,4,64]{2,1,0:T(4,128)S(1)} all-gather(f32[1,4,64]{2,1,0:T(4,128)S(1)} %get-tuple-element.56), channel_id=1, replica_groups=mesh['grp'=8,'slab'=64] {'grp','slab'}, dimensions={0}, use_global_device_ids=true | all-gather | bytes 525312 | tf_op jit(solution)/shard_map/all_gather | solution.py:129
  1299.5 1.1 copy.71
  (176 shorter events, 41.4 us)
Async XLA Ops:
  7.2 9.0 copy-start
  7.2 10.0 copy-start.2
  7.2 609.0 %all-reduce.11.cloned.1.call-start = ((), (), s32[]{:S(2)}) async-start(), calls=%async_computation | async-start | bytes 2097152
  8.0 9.4 collective-permute-start
  9.3 8.0 collective-permute-start.1
  16.2 0.8 copy-start.1
  16.3 0.7 copy-start.7
  17.4 12.4 collective-permute-start.2
  26.1 3.7 collective-permute-start.3
  29.6 0.9 copy-start.3
  29.6 1.0 copy-start.4
  30.7 3.4 collective-permute-start.5
  32.7 4.5 collective-permute-start.4
  37.2 8.1 collective-permute-start.6
  41.1 4.5 collective-permute-start.7
  137.8 0.7 copy-start.6
  137.8 0.7 copy-start.8
  385.9 230.4 %copy-start.5 = (f32[4,64]{1,0:T(4,128)S(1)}, f32[4,64]{1,0:T(4,128)}, u32[]{:S(2)}) copy-start(f32[4,64]{1,0:T(4,128)} %param.19) | copy-start | bytes 3076
Sparse Core Ops, SparseCore 0:
  138.0 478.2 all-reduce.10
where the time goes:
time: 1310 us
  blocking collectives  928 us (71%)
  waiting for transfers between devices  233 us (18%)
  local copies, waits for them, and re-layouts  74 us (6%)
  starting transfers between devices  27.2 us (2%)
  matrix products  23.4 us (2%)
  between operations  14.5 us (1%)
    all_gather x1, blocking collectives, local(): lax.all_gather(updated_rows, ('grp', 'slab'), axis=0, tiled=True)  682 us
    unnamed x2, waiting for transfers between devices  230 us
    unnamed x1, blocking collectives  135 us
    psum x1, blocking collectives, local(): grad_dense = lax.psum(grad_dense, ('grp', 'slab'))  111 us
    gather x128, local copies, waits for them, and re-layouts  64.1 us
  transfers between devices with their start and end apart: 9, of which 3 were waited for; matrix products, arithmetic and copies ran while one was open for 1% of the time, Pallas kernels for 0%

commit v1 on v0

v1 whole, which is shorter than its diff:
```python
import jax
import jax.numpy as jnp
import numpy as np
from jax import lax
from jax.experimental import pallas as pl
from jax.experimental.pallas import tpu as pltpu
from jax.sharding import PartitionSpec as P

SUB = 128
MODES = 16
WIDTH = 64
LINES = 16
NG = 8
NS = 64
NZ = 16
PEERS = 32
TOTAL = 8192

decay_rate = 0.9
learn_rate = 0.5
dense_rate = 3.0

MESH = pl.DeviceIdType.MESH
F32 = jnp.float32
HIGHEST = lax.Precision.HIGHEST
GELU_C = float(np.sqrt(2.0 / np.pi))

LANE_P = 0
LANE_M1 = 32
LANE_Q = 40
LANE_M0 = 72
LANE_PROJ = 80
LANE_LOSS = 88


def tables():
    s = np.arange(SUB)[None, :]
    k = np.arange(MODES)[:, None]
    angle = (k * s % SUB) * (2.0 * np.pi / SUB)
    cos, sin = np.cos(angle), np.sin(angle)
    weight = np.where(k == 0, 1.0, 2.0) / SUB
    er, ei = cos.sum(1, keepdims=True), -sin.sum(1, keepdims=True)
    a0 = weight * (er * cos - ei * sin)
    b0 = -weight * (ei * cos + er * sin)
    tail = np.zeros((8, SUB))
    tail[0] = 1.0
    return np.concatenate([cos, -sin, weight * cos, weight * sin, a0, b0, tail]).astype(np.float32)


def nt(a, b):
    return lax.dot_general(a, b, (((1,), (1,)), ((), ())), precision=HIGHEST, preferred_element_type=F32)


def nn(a, b):
    return lax.dot_general(a, b, (((1,), (0,)), ((), ())), precision=HIGHEST, preferred_element_type=F32)


def iota(shape, dim):
    return lax.broadcasted_iota(jnp.int32, shape, dim)


def take_lanes(x, index):
    return jnp.take_along_axis(x, index, axis=1, mode="promise_in_bounds")


def stencil(mid, others, rate, forc):
    beside = others[0] + others[1] + others[2] + others[3]
    beside = beside + pltpu.roll(mid, 1, axis=1) + pltpu.roll(mid, mid.shape[1] - 1, axis=1)
    return rate * (beside - 6.0 * mid) + forc


def kernel(
    vel, rate, forc, aline, az, assign, spec, dense, mom, tab,
    field_o, loss_o, spec_o, dense_o, mom_o,
    vel_v, rate_v, forc_v, asg_v, spec_v, dense_v, tab_v,
    side_snd, side_rcv, corn_snd, corn_rcv,
    v1_s, chg_s, fld_s, samp, diff_s, right, dp_s,
    pairb, zb, bun, gath, base_s, grad_s, out_s, dout_s, mout_s, lout_s,
    pay, rsb, zrb, agb,
    ld, st, ssem, rsem,
):
    g = lax.axis_index("grp")
    s = lax.axis_index("slab")
    z = s // 4
    xc = lax.rem(s, 4)
    xh = xc // 2
    c = lax.rem(xc, 2)
    me = g * 4 + xc
    xy = g * 2 + xh
    d = g * NS + s

    barrier = pltpu.get_barrier_semaphore()

    def greet(device):
        pl.semaphore_signal(barrier, inc=1, device_id=device, device_id_type=MESH)

    def plane_peer(i):
        p = lax.rem(me + i, PEERS)
        return p, (p // 4, z * 4 + lax.rem(p, 4))

    def z_peer(i):
        zz = lax.rem(z + i, NZ)
        return zz, (g, zz * 4 + xc)

    def xy_peer(i):
        p = lax.rem(xy + i, 16)
        return p, (p // 2, z * 4 + lax.rem(p, 2) * 2 + c)

    up_g, dn_g = lax.rem(g + 1, NG), lax.rem(g + NG - 1, NG)
    up_s, dn_s = lax.rem(s + 1, NS), lax.rem(s + NS - 1, NS)
    sides = [(up_g, s), (dn_g, s), (g, up_s), (g, dn_s)]
    corners = [(up_g, up_s), (up_g, dn_s), (dn_g, up_s), (dn_g, dn_s)]
    partner = (g, s + 1 - 2 * c)

    loads = []
    for i, (src, dst) in enumerate(
        [
            (vel, vel_v),
            (rate, rate_v),
            (forc, forc_v),
            (mom, pairb.at[c]),
            (spec, spec_v),
            (dense, dense_v),
            (tab, tab_v),
            (assign, asg_v),
        ]
    ):
        loads.append(pltpu.make_async_copy(src, dst, ld.at[i]))
        loads[-1].start()

    def greet_plane(i, carry):
        greet(plane_peer(i)[1])
        return carry

    def greet_z(i, carry):
        greet(z_peer(i)[1])
        return carry

    for device in sides + corners:
        greet(device)
    lax.fori_loop(1, PEERS, greet_plane, 0)
    lax.fori_loop(1, NZ, greet_z, 0)

    for i in range(4):
        loads[i].wait()

    for n, (a, b) in enumerate([(7, 6), (0, 1)]):
        side_snd[n, 0] = vel_v[a]
        side_snd[n, 1] = vel_v[b]
        side_snd[n, 2] = rate_v[a]
        side_snd[n, 3] = forc_v[a]
        side_snd[2 + n, 0] = vel_v[:, a, :]
        side_snd[2 + n, 1] = vel_v[:, b, :]
        side_snd[2 + n, 2] = rate_v[:, a, :]
        side_snd[2 + n, 3] = forc_v[:, a, :]
    for n, (a, b) in enumerate([(7, 7), (7, 0), (0, 7), (0, 0)]):
        corn_snd[n] = vel_v[a, b : b + 1, :]

    pl.semaphore_wait(barrier, 8 + PEERS - 1 + NZ - 1)

    def send(src, dst, n, device):
        return pltpu.make_async_remote_copy(
            src_ref=src, dst_ref=dst, send_sem=ssem.at[n], recv_sem=rsem.at[n], device_id=device, device_id_type=MESH
        )

    for n in range(4):
        send(side_snd.at[n], side_rcv.at[n], 0, sides[n]).start()
    for n in range(4):
        send(corn_snd.at[n], corn_rcv.at[n], 1, corners[n]).start()
    send(pairb.at[c], pairb.at[c], 2, partner).start()

    for i in range(4, 8):
        loads[i].wait()
    dv = dense_v[...]
    mixing = dv[:, 0:WIDTH]
    eye = iota((WIDTH, WIDTH), 0) == iota((WIDTH, WIDTH), 1)
    gain_row = jnp.sum(jnp.where(eye, dv[:, 64:65], 0.0), axis=0, keepdims=True)
    bias_row = jnp.sum(jnp.where(eye, dv[:, 65:66], 0.0), axis=0, keepdims=True)
    gain_lanes = jnp.concatenate([gain_row, gain_row], axis=1)
    bias_lanes = jnp.concatenate([bias_row, bias_row], axis=1)
    layer_bias = dv[:, 66:67]
    proj = dv[:, 67:68]
    m1 = jnp.sum(mixing * gain_row, axis=1, keepdims=True)
    m0 = jnp.sum(mixing * bias_row, axis=1, keepdims=True) + layer_bias
    weights = spec_v[...]
    segment = jnp.where(iota((40, 2048), 1) // WIDTH == iota((40, 2048), 0), 1.0, 0.0)
    gain_tiled = jnp.concatenate([gain_lanes] * 16, axis=1)
    bias_tiled = jnp.concatenate([bias_lanes] * 16, axis=1)
    lane40 = iota((WIDTH, 40), 1)
    left1 = jnp.where(lane40 == LANE_M1, m1, nt(weights * gain_tiled, segment))
    left0 = jnp.where(lane40 == LANE_M1, m0, nt(weights * bias_tiled, segment))
    left = jnp.concatenate([left1, left0], axis=1)

    send(pairb.at[1 - c], pairb.at[1 - c], 2, partner).wait_recv()
    zb[z] = jnp.concatenate([pairb[0], pairb[1]], axis=0)

    def send_z(i, carry):
        send(zb.at[z], zb.at[z], 3, z_peer(i)[1]).start()
        return carry

    lax.fori_loop(1, NZ, send_z, 0)

    right[32:40, :] = jnp.zeros((8, 2048), F32)
    for t in range(LINES):
        right[40:80, SUB * t : SUB * (t + 1)] = tab_v[64:104, :]

    send(side_snd, side_rcv, 0, partner).wait_recv()
    send(corn_snd, corn_rcv, 1, partner).wait_recv()
    has = [g > 0, g < NG - 1, s > 0, s < NS - 1]
    planes = [[jnp.where(has[n], side_rcv[n, i], 0.0) for i in range(4)] for n in range(4)]
    corner = [
        jnp.where(jnp.logical_and(has[a], has[b]), corn_rcv[n], 0.0)
        for n, (a, b) in enumerate([(0, 2), (0, 3), (1, 2), (1, 3)])
    ]
    row = iota((8, 512), 0)

    def shifted(plane, before, after):
        lo = jnp.where(row == 0, before, pltpu.roll(plane, 1, axis=0))
        hi = jnp.where(row == 7, after, pltpu.roll(plane, 7, axis=0))
        return lo, hi

    ring = []
    for n in range(4):
        mid, far, r, f = planes[n]
        if n == 0:
            ends, own = (corner[0], corner[1]), vel_v[0]
        elif n == 1:
            ends, own = (corner[2], corner[3]), vel_v[7]
        elif n == 2:
            ends, own = (corner[0], corner[2]), vel_v[:, 0, :]
        else:
            ends, own = (corner[1], corner[3]), vel_v[:, 7, :]
        lo, hi = shifted(mid, *ends)
        ring.append(mid + stencil(mid, (far, own, lo, hi), r, f))

    def flow(cells, edge, x):
        mid = cells[x]
        below = edge[0] if x == 0 else cells[x - 1]
        above = edge[1] if x == 7 else cells[x + 1]
        lo, hi = shifted(mid, edge[2][x : x + 1, :], edge[3][x : x + 1, :])
        return mid, stencil(mid, (above, below, hi, lo), rate_v[x], forc_v[x])

    first = [vel_v[x] for x in range(8)]
    edge0 = [planes[n][0] for n in range(4)]
    second = []
    for x in range(8):
        mid, change = flow(first, edge0, x)
        second.append(mid + change)
        v1_s[8 * x : 8 * x + 8, :] = second[x]
    for x in range(8):
        mid, change = flow(second, ring, x)
        chg_s[8 * x : 8 * x + 8, :] = change
        fld_s[x] = mid + change
    field_copy = pltpu.make_async_copy(fld_s, field_o, st.at[0])
    field_copy.start()

    def wait_many(buf, count, n):
        send(buf.at[pl.ds(0, count)], buf.at[pl.ds(0, count)], n, partner).wait_recv()

    wait_many(zb, NZ - 1, 3)
    bun[...] = zb[...].reshape(128, WIDTH).T
    gath[c, xy] = bun[pl.ds(pl.multiple_of(c * 32, 32), 32), :]

    def send_xy(i, carry):
        send(gath.at[c, xy], gath.at[c, xy], 4, xy_peer(i)[1]).start()
        return carry

    lax.fori_loop(1, 16, send_xy, 0)

    row16 = iota((8, SUB), 0)
    for t in range(LINES):
        line = aline[t]
        samp[t : t + 1, :] = v1_s[pl.ds(line, 1), :]
        samp[LINES + t : LINES + t + 1, :] = chg_s[pl.ds(line, 1), :]
    windows = []
    for tile in range(4):
        start = jnp.zeros((8, SUB), jnp.int32)
        for i in range(8):
            start = jnp.where(row16 == i, az[(tile % 2) * 8 + i], start)
        block, shift = start // SUB, start % SUB
        quarter = [samp[8 * tile : 8 * tile + 8, SUB * q : SUB * (q + 1)] for q in range(4)]
        lo = jnp.where(block == 0, quarter[0], jnp.where(block == 1, quarter[1], jnp.where(block == 2, quarter[2], quarter[3])))
        hi = jnp.where(block == 0, quarter[1], jnp.where(block == 1, quarter[2], quarter[3]))
        at = iota((8, SUB), 1) + shift
        index = at % SUB
        windows.append(jnp.where(at < SUB, take_lanes(lo, index), take_lanes(hi, index)))
    inputs = jnp.concatenate(windows[:2], axis=0)
    targets = jnp.concatenate(windows[2:], axis=0)

    spectrum = nt(tab_v[0:32, :], inputs)
    cos_w, sin_w = tab_v[32:48, :], tab_v[48:64, :]
    scale = 1.0 / (TOTAL * SUB)
    proj_grad = jnp.zeros((WIDTH, SUB), F32)
    for pair in range(LINES // 2):
        cols = slice(2 * SUB * pair, 2 * SUB * (pair + 1))
        for half in range(2):
            t = 2 * pair + half
            one = slice(SUB * t, SUB * (t + 1))
            ur, ui = spectrum[0:16, t : t + 1], spectrum[16:32, t : t + 1]
            right[0:16, one] = ur * cos_w - ui * sin_w
            right[16:32, one] = -(ui * cos_w + ur * sin_w)
            right[32:33, one] = inputs[t : t + 1, :]
        pre = nn(left, right[:, cols])
        square = pre * pre
        bend = jnp.tanh(GELU_C * (pre + 0.044715 * (square * pre)))
        half_up = 0.5 * (1.0 + bend)
        hidden = pre * half_up
        slope = half_up + 0.5 * pre * (1.0 - bend * bend) * (GELU_C * (1.0 + 3.0 * 0.044715 * square))
        guess = jnp.sum(hidden * proj, axis=0, keepdims=True)
        target = jnp.concatenate([targets[2 * pair : 2 * pair + 1, :], targets[2 * pair + 1 : 2 * pair + 2, :]], axis=1)
        miss = guess - target
        diff_s[2 * pair : 2 * pair + 1, :] = miss[:, 0:SUB]
        diff_s[2 * pair + 1 : 2 * pair + 2, :] = miss[:, SUB:]
        dq = (2.0 * scale) * miss
        dpre = slope * proj * dq
        dp_s[:, cols] = dpre
        back = hidden * dq
        proj_grad = proj_grad + back[:, 0:SUB] + back[:, SUB:]
    grads = nt(dp_s[...], right[...])

    diff = diff_s[...]
    err = jnp.sum(diff * diff, axis=1, keepdims=True)
    eye16 = iota((LINES, LINES), 0) == iota((LINES, LINES), 1)
    err_row = jnp.sum(jnp.where(eye16, err, 0.0), axis=0, keepdims=True)
    named = iota((NS, LINES), 0) == asg_v[...]
    loss = jnp.sum(jnp.where(named, err_row, 0.0), axis=1, keepdims=True) / (LINES * SUB)

    lane48 = iota((WIDTH, 48), 1)
    extra = jnp.where(lane48 == LANE_PROJ - 80, jnp.sum(proj_grad, axis=1, keepdims=True), 0.0)
    extra = jnp.where(lane48 == LANE_LOSS - 80 + g, loss, extra)
    payload = jnp.concatenate([grads, extra], axis=1)
    for p in range(PEERS):
        pay[p] = payload[2 * p : 2 * p + 2, :]

    def send_scatter(i, carry):
        p, device = plane_peer(i)
        send(pay.at[p], rsb.at[me], 5, device).start()
        return carry

    lax.fori_loop(1, PEERS, send_scatter, 0)
    rsb[me] = pay[me]

    wait_many(gath.at[c], 15, 4)
    send(gath.at[c], gath.at[c], 8, partner).start()

    wait_many(rsb, PEERS - 1, 5)
    zrb[z] = jnp.sum(rsb[...], axis=0)

    def send_line(i, carry):
        send(zrb.at[z], zrb.at[z], 6, z_peer(i)[1]).start()
        return carry

    lax.fori_loop(1, NZ, send_line, 0)

    send(gath.at[1 - c], gath.at[1 - c], 8, partner).wait_recv()
    lane = iota((WIDTH, SUB), 1)
    for j in range(16):
        cols = slice(SUB * j, SUB * (j + 1))
        index = (j % 2) * 64 + (lane // 16) * 8 + lane % 8
        both = [
            take_lanes(jnp.concatenate([gath[0, (j // 2) * 2 + h], gath[1, (j // 2) * 2 + h]], axis=0), index)
            for h in range(2)
        ]
        moved = jnp.where((lane // 8) % 2 == 0, both[0], both[1])
        base_s[:, cols] = spec_v[:, cols] - (learn_rate * decay_rate) * moved

    wait_many(zrb, NZ - 1, 6)
    agb[me] = jnp.sum(zrb[...], axis=0)

    def send_gather(i, carry):
        send(agb.at[me], agb.at[me], 7, plane_peer(i)[1]).start()
        return carry

    lax.fori_loop(1, PEERS, send_gather, 0)
    wait_many(agb, PEERS - 1, 7)
    total = jnp.concatenate([agb[p] for p in range(PEERS)], axis=0)

    gain_back = jnp.zeros((WIDTH, SUB), F32)
    bias_back = jnp.zeros((WIDTH, SUB), F32)
    stores = []
    for j in range(16):
        cols = slice(SUB * j, SUB * (j + 1))
        index = jnp.where(lane < 64, 2 * j, 2 * j + 1)
        by_gain = take_lanes(total, index + LANE_P)
        by_bias = take_lanes(total, index + LANE_Q)
        grad = gain_lanes * by_gain + bias_lanes * by_bias
        grad_s[:, cols] = grad
        out_s[:, cols] = base_s[:, cols] - learn_rate * grad
        w = spec_v[:, cols]
        gain_back = gain_back + by_gain * w
        bias_back = bias_back + by_bias * w
        if j % 4 == 3:
            some = pl.ds(SUB * (j - 3), SUB * 4)
            stores.append(pltpu.make_async_copy(out_s.at[:, some], spec_o.at[:, some], st.at[1 + j // 4]))
            stores[-1].start()

    dm1, dm0 = total[:, LANE_M1 : LANE_M1 + 1], total[:, LANE_M0 : LANE_M0 + 1]

    def to_column(back, dm):
        both = jnp.sum(back, axis=0, keepdims=True)
        both = both[:, 0:WIDTH] + both[:, WIDTH:] + jnp.sum(mixing * dm, axis=0, keepdims=True)
        return jnp.sum(jnp.where(eye, both, 0.0), axis=1, keepdims=True)

    dout_s[:, 0:64] = mixing - dense_rate * (gain_row * dm1 + bias_row * dm0)
    dout_s[:, 64:65] = dv[:, 64:65] - dense_rate * to_column(gain_back, dm1)
    dout_s[:, 65:66] = dv[:, 65:66] - dense_rate * to_column(bias_back, dm0)
    dout_s[:, 66:67] = layer_bias - dense_rate * dm0
    dout_s[:, 67:68] = proj - dense_rate * total[:, LANE_PROJ : LANE_PROJ + 1]
    stores.append(pltpu.make_async_copy(dout_s, dense_o, st.at[5]))
    stores[-1].start()

    mine = grad_s[:, pl.ds(pl.multiple_of((d // 32) * SUB, SUB), SUB)]
    mine = pltpu.roll(mine, lax.rem(SUB - lax.rem(d, 32) * 4, SUB), axis=1)
    mout_s[...] = decay_rate * pairb[c] + mine.T[0:4, :]
    stores.append(pltpu.make_async_copy(mout_s, mom_o, st.at[6]))
    stores[-1].start()

    own = jnp.logical_and(iota((NS, SUB), 0) == s, lane == LANE_LOSS + g)
    own = jnp.sum(jnp.where(own, total, 0.0), axis=1, keepdims=True)
    lout_s[...] = jnp.sum(own, axis=0, keepdims=True)
    stores.append(pltpu.make_async_copy(lout_s, loss_o, st.at[7]))
    stores[-1].start()

    field_copy.wait()
    for copy in stores:
        copy.wait()
    send(side_snd, side_rcv, 0, partner).wait_send()
    send(corn_snd, corn_rcv, 1, partner).wait_send()
    send(pairb.at[c], pairb.at[c], 2, partner).wait_send()

    def sent(buf, count, n):
        send(buf.at[pl.ds(0, count)], buf.at[pl.ds(0, count)], n, partner).wait_send()

    sent(zb, NZ - 1, 3)
    sent(gath.at[c], 15, 4)
    sent(pay, PEERS - 1, 5)
    sent(zrb, NZ - 1, 6)
    sent(agb, PEERS - 1, 7)
    send(gath.at[c], gath.at[c], 8, partner).wait_send()


def local(velocity, rate, forcing, anchor_line, anchor_z, assign, spectral, dense, momentum):
    smem = pl.BlockSpec(memory_space=pltpu.SMEM)
    anyw = pl.BlockSpec(memory_space=pl.ANY)
    vmem = pltpu.VMEM
    field, loss, spec, dens, mom = pl.pallas_call(
        kernel,
        out_shape=(
            jax.ShapeDtypeStruct((8, 8, 512), F32),
            jax.ShapeDtypeStruct((1, 1), F32),
            jax.ShapeDtypeStruct((WIDTH, 2048), F32),
            jax.ShapeDtypeStruct((WIDTH, 68), F32),
            jax.ShapeDtypeStruct((4, WIDTH), F32),
        ),
        in_specs=[anyw, anyw, anyw, smem, smem, anyw, anyw, anyw, anyw, anyw],
        out_specs=(anyw, anyw, anyw, anyw, anyw),
        scratch_shapes=[
            vmem((8, 8, 512), F32),
            vmem((8, 8, 512), F32),
            vmem((8, 8, 512), F32),
            vmem((1, LINES), jnp.int32),
            vmem((WIDTH, 2048), F32),
            vmem((WIDTH, 68), F32),
            vmem((104, SUB), F32),
            vmem((4, 4, 8, 512), F32),
            vmem((4, 4, 8, 512), F32),
            vmem((4, 1, 512), F32),
            vmem((4, 1, 512), F32),
            vmem((64, 512), F32),
            vmem((64, 512), F32),
            vmem((8, 8, 512), F32),
            vmem((2 * LINES, 512), F32),
            vmem((LINES, SUB), F32),
            vmem((80, 2048), F32),
            vmem((WIDTH, 2048), F32),
            vmem((2, 4, WIDTH), F32),
            vmem((NZ, 8, WIDTH), F32),
            vmem((WIDTH, SUB), F32),
            vmem((2, 16, 32, SUB), F32),
            vmem((WIDTH, 2048), F32),
            vmem((WIDTH, 2048), F32),
            vmem((WIDTH, 2048), F32),
            vmem((WIDTH, 68), F32),
            vmem((4, WIDTH), F32),
            vmem((1, 1), F32),
            vmem((PEERS, 2, SUB), F32),
            vmem((PEERS, 2, SUB), F32),
            vmem((NZ, 2, SUB), F32),
            vmem((PEERS, 2, SUB), F32),
            pltpu.SemaphoreType.DMA((8,)),
            pltpu.SemaphoreType.DMA((8,)),
            pltpu.SemaphoreType.DMA((9,)),
            pltpu.SemaphoreType.DMA((9,)),
        ],
        compiler_params=pltpu.CompilerParams(
            collective_id=0, has_side_effects=True, vmem_limit_bytes=32 * 1024 * 1024
        ),
    )(velocity, rate, forcing, anchor_line, anchor_z, assign.T, spectral.T, dense.T, momentum, jnp.asarray(tables()))
    return (field, loss, spec.T, dens.T, mom)


def solution(mesh):
    placed = (
        P("grp", "slab", None),
        P("grp", "slab", None),
        P("grp", "slab", None),
        P(("grp", "slab")),
        P(("grp", "slab")),
        P(("grp", "slab"), None),
        P(),
        P(),
        P(("grp", "slab"), None),
    )
    return jax.shard_map(
        local,
        mesh=mesh,
        in_specs=placed,
        out_specs=(P("grp", "slab", None), P("grp", "slab"), P(), P(), P(("grp", "slab"), None)),
        check_vma=False,
    )
```

time: 1310 us -> 62.3 us (0.05)
  blocking collectives: 928 us -> 0 us
  waiting for transfers between devices: 233 us -> 0 us
  local copies, waits for them, and re-layouts: 74 us -> 8.63 us
  Pallas kernels: 0 us -> 50.9 us
  starting transfers between devices: 27.2 us -> 0 us
  matrix products: 23.4 us -> 0 us
    all_gather x1 -> x0, blocking collectives: 682 us -> none  [local(): lax.all_gather(updated_rows, ('grp', 'slab'), axis=0, tiled=True)]
    unnamed x2 -> x0, waiting for transfers between devices: 230 us -> none
    unnamed x1 -> x0, blocking collectives: 135 us -> none
    psum x1 -> x0, blocking collectives: 111 us -> none  [local(): grad_dense = lax.psum(grad_dense, ('grp', 'slab'))]
    gather x130 -> x0, local copies, waits for them, and re-layouts: 65.2 us -> none
    pallas_call x0 -> x1, Pallas kernels: none -> 50.9 us  [local(): pl.pallas_call(kernel, out_shape=(jax.ShapeDtypeStruct((8, 8, 512), F32),...]
    ppermute x8 -> x0, starting transfers between devices: 27.2 us -> none  [the longest x4 15.1 us: extended(): lax.ppermute(head, axis, [((i + 1) % count, i) for i in range(ends)])]
    dot_general x26 -> x0, matrix products: 23.4 us -> none  [the longest x3 2.72 us: line_errors(): jnp.einsum('bwk,kwv->bvk', imag_in, w_imag, precision=highest)]
  transfers between devices with their start and end apart: 9 -> 0, of which waited for: 3 -> 0; matrix products, arithmetic and copies ran while one was open for 1% -> 0% of each run, Pallas kernels for 0% -> 0%
where the time goes in v1:
time: 62.3 us; the launch traced here: 62 us
  Pallas kernels  50.9 us (82%)
  local copies, waits for them, and re-layouts  8.63 us (14%)
  between operations  2.45 us (4%)
    pallas_call x1, Pallas kernels, local(): pl.pallas_call(kernel, out_shape=(jax.ShapeDtypeStruct((8, 8, 512), F32),...  50.9 us
    unnamed x24, local copies, waits for them, and re-layouts  8.63 us

profile of v1, /device:TPU:1, one launch (start us, length us, event | category | flops | bytes accessed | tf_op | source)
XLA Modules:
  0.0 62.0 jit_solution(8755488909440732947)
XLA Ops:
  0.6 0.0 copy-start.6
  0.6 0.0 copy-start.7
  0.7 0.0 copy-start.8
  0.7 0.0 copy-start.9
  0.7 0.6 %copy-done.6 = f32[4,64]{1,0:T(4,128)S(1)} copy-done((f32[4,64]{1,0:T(4,128)S(1)}, f32[4,64]{1,0:T(4,128)}, u32[]{:S(2)}) %copy-start.6) | copy-done | bytes 1048
  1.3 0.0 copy-done.7
  1.3 0.0 copy-done.8
  1.3 0.0 copy-done.9
  1.3 0.0 copy-start
  1.3 1.0 %copy-done = f32[2048,64]{0,1:T(8,128)S(1)} copy-done((f32[2048,64]{0,1:T(8,128)S(1)}, f32[2048,64]{0,1:T(8,128)}, u32[]{:S(2)}) %copy-start) | copy-done | bytes 524312
  2.4 0.0 copy-start.1
  2.4 0.9 %copy-done.1 = f32[8,8,512]{2,1,0:T(8,128)S(1)} copy-done((f32[8,8,512]{2,1,0:T(8,128)S(1)}, f32[8,8,512]{2,1,0:T(8,128)}, u32[]{:S(2)}) %copy-start.1) | copy-done | bytes 131096
  3.3 0.0 copy-start.2
  3.3 0.9 %copy-done.2 = f32[8,8,512]{2,1,0:T(8,128)S(1)} copy-done((f32[8,8,512]{2,1,0:T(8,128)S(1)}, f32[8,8,512]{2,1,0:T(8,128)}, u32[]{:S(2)}) %copy-start.2) | copy-done | bytes 131096
  4.2 0.0 copy-start.3
  4.2 0.9 %copy-done.3 = f32[8,8,512]{2,1,0:T(8,128)S(1)} copy-done((f32[8,8,512]{2,1,0:T(8,128)S(1)}, f32[8,8,512]{2,1,0:T(8,128)}, u32[]{:S(2)}) %copy-start.3) | copy-done | bytes 131096
  5.1 0.0 copy-start.4
  5.1 0.8 %copy-done.4 = f32[104,128]{1,0:T(8,128)S(1)} copy-done((f32[104,128]{1,0:T(8,128)S(1)}, f32[104,128]{1,0:T(8,128)}, u32[]{:S(2)}) %copy-start.4) | copy-done | bytes 53272
  5.9 0.0 copy-start.5
  5.9 0.8 %copy-done.5 = f32[68,64]{0,1:T(8,128)S(1)} copy-done((f32[68,64]{0,1:T(8,128)S(1)}, f32[68,64]{0,1:T(8,128)}, u32[]{:S(2)}) %copy-start.5) | copy-done | bytes 17432
  6.7 50.9 %shard_map.137 = (f32[8,8,512]{2,1,0:T(8,128)S(1)}, f32[1,1]{1,0:T(1,128)}, f32[64,2048]{1,0:T(8,128)S(1)}, f32[64,68]{1,0:T(8,128)S(1)}, f32[4,64]{1,0:T(4,128)S(1)}) custom-call(f32[8,8,512]{2,1,0:T(8,128)S(1)} %copy-done.1, f32[8,8,512]{2,1,0:T(8,128)S(1)} %copy-done.2, f32[8,8,512]{2,1,0:T(8,128)S(1)} %copy-done.3, s32[16]{0:T(128)S(1)} %copy-done.7, ...), custom_call_target="tpu_custom_call" | custom-call | tf_op jit(solution)/shard_map/pallas_call | solution.py:446
  57.5 0.7 %copy.20 = f32[8,8,512]{2,1,0:T(8,128)} copy(f32[8,8,512]{2,1,0:T(8,128)S(1)} %get-tuple-element.20) | data formatting | bytes 262144
  58.8 0.8 %copy.22 = f32[2048,64]{0,1:T(8,128)} copy(f32[2048,64]{0,1:T(8,128)S(1)} %bitcast.6) | data formatting | bytes 1048576
  59.6 0.6 copy.23
  60.3 0.6 copy.24
Async XLA Ops:
  0.6 0.7 %copy-start.6 = (f32[4,64]{1,0:T(4,128)S(1)}, f32[4,64]{1,0:T(4,128)}, u32[]{:S(2)}) copy-start(f32[4,64]{1,0:T(4,128)} %mom.1) | copy-start | bytes 3076
  0.6 0.7 %copy-start.7 = (s32[16]{0:T(128)S(1)}, s32[16]{0:T(128)}, u32[]{:S(2)}) copy-start(s32[16]{0:T(128)} %aline.1) | copy-start | bytes 196
  0.7 0.7 %copy-start.8 = (s32[16]{0:T(128)S(1)}, s32[16]{0:T(128)}, u32[]{:S(2)}) copy-start(s32[16]{0:T(128)} %az.1) | copy-start | bytes 196
  0.7 0.7 %copy-start.9 = (s32[16,1]{0,1:T(1,128)S(1)}, s32[16,1]{0,1:T(1,128)}, u32[]{:S(2)}) copy-start(s32[16,1]{0,1:T(1,128)} %param.15) | copy-start | bytes 196
  1.3 1.0 %copy-start = (f32[2048,64]{0,1:T(8,128)S(1)}, f32[2048,64]{0,1:T(8,128)}, u32[]{:S(2)}) copy-start(f32[2048,64]{0,1:T(8,128)} %param.16) | copy-start | bytes 1572868
  2.4 0.9 %copy-start.1 = (f32[8,8,512]{2,1,0:T(8,128)S(1)}, f32[8,8,512]{2,1,0:T(8,128)}, u32[]{:S(2)}) copy-start(f32[8,8,512]{2,1,0:T(8,128)} %vel.1) | copy-start | bytes 393220
  3.3 0.9 %copy-start.2 = (f32[8,8,512]{2,1,0:T(8,128)S(1)}, f32[8,8,512]{2,1,0:T(8,128)}, u32[]{:S(2)}) copy-start(f32[8,8,512]{2,1,0:T(8,128)} %rate.1) | copy-start | bytes 393220
  4.2 0.9 %copy-start.3 = (f32[8,8,512]{2,1,0:T(8,128)S(1)}, f32[8,8,512]{2,1,0:T(8,128)}, u32[]{:S(2)}) copy-start(f32[8,8,512]{2,1,0:T(8,128)} %forc.1) | copy-start | bytes 393220
  5.1 0.8 %copy-start.4 = (f32[104,128]{1,0:T(8,128)S(1)}, f32[104,128]{1,0:T(8,128)}, u32[]{:S(2)}) copy-start(f32[104,128]{1,0:T(8,128)} %constant.2.clone.tab) | copy-start | bytes 159748
  5.9 0.8 %copy-start.5 = (f32[68,64]{0,1:T(8,128)S(1)}, f32[68,64]{0,1:T(8,128)}, u32[]{:S(2)}) copy-start(f32[68,64]{0,1:T(8,128)} %param.17) | copy-start | bytes 52228

commit v2 on v1

v2 whole, which is shorter than its diff:
```python
import jax
import jax.numpy as jnp
import numpy as np
from jax import lax
from jax.experimental import pallas as pl
from jax.experimental.pallas import tpu as pltpu
from jax.sharding import PartitionSpec as P

SUB = 128
MODES = 16
WIDTH = 64
LINES = 16
NG = 8
NS = 64
NZ = 16
NXY = 16
TOTAL = 8192

decay_rate = 0.9
learn_rate = 0.5
dense_rate = 3.0

MESH = pl.DeviceIdType.MESH
F32 = jnp.float32
BF16 = jnp.bfloat16
HIGHEST = lax.Precision.HIGHEST
GELU_C = float(np.sqrt(2.0 / np.pi))

LANE_P = 0
LANE_Q = 32
LANE_M1 = 64
LANE_M0 = 65
LANE_PROJ = 66
LANE_LOSS = 72
KEEP = 80


def tables():
    s = np.arange(SUB)[None, :]
    k = np.arange(MODES)[:, None]
    angle = (k * s % SUB) * (2.0 * np.pi / SUB)
    cos, sin = np.cos(angle), np.sin(angle)
    weight = np.where(k == 0, 1.0, 2.0) / SUB
    er, ei = cos.sum(1, keepdims=True), -sin.sum(1, keepdims=True)
    a0 = weight * (er * cos - ei * sin)
    b0 = -weight * (ei * cos + er * sin)
    return np.concatenate([cos, -sin, weight * cos, weight * sin, a0, b0]).astype(np.float32)


def nt(a, b, precision=None):
    return lax.dot_general(a, b, (((1,), (1,)), ((), ())), precision=precision, preferred_element_type=F32)


def nn(a, b):
    return lax.dot_general(a, b, (((1,), (0,)), ((), ())), preferred_element_type=F32)


def parts(x):
    high = x.astype(BF16)
    return high, (x - high.astype(F32)).astype(BF16)


def iota(shape, dim):
    return lax.broadcasted_iota(jnp.int32, shape, dim)


def take_lanes(x, index):
    return jnp.take_along_axis(x, index, axis=1, mode="promise_in_bounds")


def stencil(mid, others, rate, forc):
    beside = others[0] + others[1] + others[2] + others[3]
    beside = beside + pltpu.roll(mid, 1, axis=1) + pltpu.roll(mid, mid.shape[1] - 1, axis=1)
    return rate * (beside - 6.0 * mid) + forc


def kernel(
    vel, rate, forc, aline, az, assign, spec, dense, mom, tab,
    field_o, loss_o, spec_o, dense_o, mom_o,
    vel_v, rate_v, forc_v, asg_v, spec_v, dense_v, tab_v,
    edge_snd, edge_rcv,
    v1_s, chg_s, samp, diff_s, right, dp_s,
    mz, gath, base_s, grad_s,
    pay, crs, half_s, rsb, zrb, agb,
    ld, ssem, rsem,
):
    g = lax.axis_index("grp")
    s = lax.axis_index("slab")
    z = s // 4
    xc = lax.rem(s, 4)
    xh = xc // 2
    c = lax.rem(xc, 2)
    xy = g * 2 + xh
    d = g * NS + s

    barrier = pltpu.get_barrier_semaphore()

    def greet(device):
        pl.semaphore_signal(barrier, inc=1, device_id=device, device_id_type=MESH)

    def z_peer(i):
        zz = lax.rem(z + i, NZ)
        return (g, zz * 4 + xc)

    def xy_peer(i):
        p = lax.rem(xy + i, NXY)
        return p, (p // 2, z * 4 + lax.rem(p, 2) * 2 + c)

    sides = [
        (lax.rem(g + 1, NG), s),
        (lax.rem(g + NG - 1, NG), s),
        (g, lax.rem(s + 1, NS)),
        (g, lax.rem(s + NS - 1, NS)),
    ]
    partner = (g, s + 1 - 2 * c)

    def load(src, dst, n):
        copy = pltpu.make_async_copy(src, dst, ld.at[n])
        copy.start()
        return copy

    def greet_z(i, carry):
        greet(z_peer(i))
        return carry

    def greet_xy(i, carry):
        greet(xy_peer(i)[1])
        return carry

    vel_load = load(vel, vel_v, 0)
    for device in sides:
        greet(device)
    greet(partner)
    lax.fori_loop(1, NZ, greet_z, 0, unroll=True)
    lax.fori_loop(1, NXY, greet_xy, 0, unroll=True)
    mom_load = load(mom, mz.at[z], 1)
    flow_loads = [load(rate, rate_v, 2), load(forc, forc_v, 3)]
    other_loads = [load(spec, spec_v, 4), load(dense, dense_v, 5), load(tab, tab_v, 6), load(assign, asg_v, 7)]

    def send(src, dst, n, device):
        return pltpu.make_async_remote_copy(
            src_ref=src, dst_ref=dst, send_sem=ssem.at[n], recv_sem=rsem.at[n], device_id=device, device_id_type=MESH
        )

    def arrived(buf, count, n):
        send(buf.at[pl.ds(0, count)], buf.at[pl.ds(0, count)], n, partner).wait_recv()

    def sent(buf, count, n):
        send(buf.at[pl.ds(0, count)], buf.at[pl.ds(0, count)], n, partner).wait_send()

    def send_edges(phase):
        for n in range(4):
            send(edge_snd.at[phase, n], edge_rcv.at[phase, n], phase, sides[n]).start()

    vel_load.wait()
    edge_snd[0, 0] = vel_v[7]
    edge_snd[0, 1] = vel_v[0]
    edge_snd[0, 2] = vel_v[:, 7, :]
    edge_snd[0, 3] = vel_v[:, 0, :]
    pl.semaphore_wait(barrier, 5 + NZ - 1 + NXY - 1)
    send_edges(0)

    mom_load.wait()

    def send_z(i, carry):
        send(mz.at[z], mz.at[z], 2, z_peer(i)).start()
        return carry

    lax.fori_loop(1, NZ, send_z, 0, unroll=True)

    for copy in other_loads:
        copy.wait()
    dv = dense_v[...]
    mixing = dv[:, 0:WIDTH]
    eye = iota((WIDTH, WIDTH), 0) == iota((WIDTH, WIDTH), 1)
    gain_row = jnp.sum(jnp.where(eye, dv[:, 64:65], 0.0), axis=0, keepdims=True)
    bias_row = jnp.sum(jnp.where(eye, dv[:, 65:66], 0.0), axis=0, keepdims=True)
    gain_lanes = jnp.concatenate([gain_row, gain_row], axis=1)
    bias_lanes = jnp.concatenate([bias_row, bias_row], axis=1)
    layer_bias = dv[:, 66:67]
    proj = dv[:, 67:68]
    m1 = jnp.sum(mixing * gain_row, axis=1, keepdims=True)
    m0 = jnp.sum(mixing * bias_row, axis=1, keepdims=True) + layer_bias
    weights = spec_v[...]
    segment = jnp.where(iota((32, 2048), 1) // WIDTH == iota((32, 2048), 0), 1.0, 0.0).astype(BF16)
    gain_high, gain_low = parts(weights * jnp.concatenate([gain_lanes] * 16, axis=1))
    bias_high, bias_low = parts(weights * jnp.concatenate([bias_lanes] * 16, axis=1))
    seen = nt(jnp.concatenate([gain_high, gain_low, bias_high, bias_low], axis=0), segment)
    lane16 = iota((WIDTH, 16), 1)
    left = jnp.concatenate(
        [
            seen[0:64] + seen[64:128],
            seen[128:192] + seen[192:256],
            jnp.where(lane16 == 0, m1, jnp.where(lane16 == 1, m0, 0.0)),
        ],
        axis=1,
    )
    left_high, left_low = parts(left)
    left3 = jnp.concatenate([left_high, left_high, left_low], axis=1)
    for row0, part in zip((32, 112, 192), [parts(tab_v[64:96, :])[i] for i in (0, 1, 0)]):
        for t in range(LINES):
            right[row0 : row0 + 32, SUB * t : SUB * (t + 1)] = part

    has = [g > 0, g < NG - 1, s > 0, s < NS - 1]
    row = iota((8, 512), 0)

    def flow(cells, phase):
        edge = [jnp.where(has[n], edge_rcv[phase, n], 0.0) for n in range(4)]
        changes = []
        for x in range(8):
            mid = cells[x]
            below = edge[0] if x == 0 else cells[x - 1]
            above = edge[1] if x == 7 else cells[x + 1]
            left_of = jnp.where(row == 0, edge[2][x : x + 1, :], pltpu.roll(mid, 1, axis=0))
            right_of = jnp.where(row == 7, edge[3][x : x + 1, :], pltpu.roll(mid, 7, axis=0))
            beside = above + below + right_of + left_of
            beside = beside + pltpu.roll(mid, 1, axis=1) + pltpu.roll(mid, 511, axis=1)
            changes.append(rate_v[x] * (beside - 6.0 * mid) + forc_v[x])
        return changes

    for copy in flow_loads:
        copy.wait()
    arrived(edge_rcv.at[0], 4, 0)
    first = [vel_v[x] for x in range(8)]
    second = [mid + change for mid, change in zip(first, flow(first, 0))]
    edge_snd[1, 0] = second[7]
    edge_snd[1, 1] = second[0]
    edge_snd[1, 2] = jnp.concatenate([p[7:8, :] for p in second], axis=0)
    edge_snd[1, 3] = jnp.concatenate([p[0:1, :] for p in second], axis=0)
    send_edges(1)
    for x in range(8):
        v1_s[8 * x : 8 * x + 8, :] = second[x]

    arrived(mz, NZ - 1, 2)
    turned = jnp.concatenate([mz[i] for i in range(NZ)], axis=0).T
    gath[c, xy] = jnp.concatenate([turned[0:32, :], turned[32:64, :]], axis=1)

    def send_xy(i, carry):
        send(gath.at[c, xy], gath.at[c, xy], 3, xy_peer(i)[1]).start()
        return carry

    lax.fori_loop(1, NXY, send_xy, 0, unroll=True)

    for t in range(LINES):
        samp[t : t + 1, :] = v1_s[pl.ds(aline[t], 1), :]
    row8 = iota((8, SUB), 0)

    def windows(tile):
        start = jnp.zeros((8, SUB), jnp.int32)
        for i in range(8):
            start = jnp.where(row8 == i, az[(tile % 2) * 8 + i], start)
        block, shift = start // SUB, start % SUB
        quarter = [samp[8 * tile : 8 * tile + 8, SUB * q : SUB * (q + 1)] for q in range(4)]
        lo = jnp.where(block == 0, quarter[0], jnp.where(block == 1, quarter[1], jnp.where(block == 2, quarter[2], quarter[3])))
        hi = jnp.where(block == 0, quarter[1], jnp.where(block == 1, quarter[2], quarter[3]))
        at = iota((8, SUB), 1) + shift
        index = at % SUB
        return jnp.where(at < SUB, take_lanes(lo, index), take_lanes(hi, index))

    inputs = jnp.concatenate([windows(0), windows(1)], axis=0)
    spectrum = nt(tab_v[0:32, :], inputs, HIGHEST)
    cos_w, sin_w = tab_v[32:48, :], tab_v[48:64, :]
    row16 = iota((16, SUB), 0)
    for t in range(LINES):
        one = slice(SUB * t, SUB * (t + 1))
        ur, ui = spectrum[0:16, t : t + 1], spectrum[16:32, t : t + 1]
        waves = jnp.concatenate([ur * cos_w - ui * sin_w, -(ui * cos_w + ur * sin_w)], axis=0)
        high, low = parts(waves)
        right[0:32, one] = high
        right[80:112, one] = low
        right[160:192, one] = high
        rest = jnp.where(row16 == 0, inputs[t : t + 1, :], jnp.where(row16 == 1, 1.0, 0.0))
        high, low = parts(rest)
        right[64:80, one] = high
        right[144:160, one] = low
        right[224:240, one] = high

    arrived(edge_rcv.at[1], 4, 1)
    for x, change in enumerate(flow(second, 1)):
        chg_s[8 * x : 8 * x + 8, :] = change
        field_o[x] = second[x] + change
    for t in range(LINES):
        samp[LINES + t : LINES + t + 1, :] = chg_s[pl.ds(aline[t], 1), :]
    targets = jnp.concatenate([windows(2), windows(3)], axis=0)

    scale = 1.0 / (TOTAL * SUB)
    proj_grad = jnp.zeros((WIDTH, SUB), F32)
    for pair in range(LINES // 2):
        cols = slice(2 * SUB * pair, 2 * SUB * (pair + 1))
        pre = nn(left3, right[:, cols])
        square = pre * pre
        bend = jnp.tanh(GELU_C * (pre + 0.044715 * (square * pre)))
        half_up = 0.5 * (1.0 + bend)
        hidden = pre * half_up
        slope = half_up + 0.5 * pre * (1.0 - bend * bend) * (GELU_C * (1.0 + 3.0 * 0.044715 * square))
        guess = jnp.sum(hidden * proj, axis=0, keepdims=True)
        target = jnp.concatenate([targets[2 * pair : 2 * pair + 1, :], targets[2 * pair + 1 : 2 * pair + 2, :]], axis=1)
        miss = guess - target
        diff_s[2 * pair : 2 * pair + 1, :] = miss[:, 0:SUB]
        diff_s[2 * pair + 1 : 2 * pair + 2, :] = miss[:, SUB:]
        dq = (2.0 * scale) * miss
        high, low = parts(slope * proj * dq)
        dp_s[0:64, cols] = high
        dp_s[64:128, cols] = low
        back = hidden * dq
        proj_grad = proj_grad + back[:, 0:SUB] + back[:, SUB:]
    grads = nt(dp_s[...], right[0:160, :])
    grads = grads[0:64, 0:KEEP] + grads[0:64, KEEP:] + grads[64:128, 0:KEEP]

    diff = diff_s[...]
    err = jnp.sum(diff * diff, axis=1, keepdims=True)
    eye16 = iota((LINES, LINES), 0) == iota((LINES, LINES), 1)
    err_row = jnp.sum(jnp.where(eye16, err, 0.0), axis=0, keepdims=True)
    named = iota((NS, LINES), 0) == asg_v[...]
    loss = jnp.sum(jnp.where(named, err_row, 0.0), axis=1, keepdims=True) / (LINES * SUB)

    keep = iota((WIDTH, KEEP), 1)
    grads = jnp.where(keep == LANE_PROJ, jnp.sum(proj_grad, axis=1, keepdims=True), grads)
    grads = jnp.where(keep == LANE_LOSS + g, loss, grads)
    payload = jnp.concatenate([grads, jnp.zeros((WIDTH, SUB - KEEP), F32)], axis=1)
    for h in range(2):
        for p in range(NXY):
            pay[h, p] = payload[32 * h + 2 * p : 32 * h + 2 * p + 2, :]

    send(pay.at[1 - c], crs, 4, partner).start()

    arrived(gath.at[c], NXY - 1, 3)
    send(gath.at[c], gath.at[c], 5, partner).start()

    send(pay.at[1 - c], crs, 4, partner).wait_recv()
    half_s[...] = pay[c] + crs[...]

    def send_scatter(i, carry):
        p, device = xy_peer(i)
        send(half_s.at[p], rsb.at[xy], 6, device).start()
        return carry

    lax.fori_loop(1, NXY, send_scatter, 0, unroll=True)
    rsb[xy] = half_s[xy]
    arrived(rsb, NXY - 1, 6)
    zrb[z] = jnp.sum(rsb[...], axis=0)

    def send_line(i, carry):
        send(zrb.at[z], zrb.at[z], 7, z_peer(i)).start()
        return carry

    lax.fori_loop(1, NZ, send_line, 0, unroll=True)

    send(gath.at[1 - c], gath.at[1 - c], 5, partner).wait_recv()
    lane32 = iota((32, SUB), 1)
    for j in range(16):
        for v in range(2):
            index = v * 64 + ((j % 2) * 8 + lane32 // 16) * 4 + lane32 % 4
            four = [take_lanes(gath[k % 2, (j // 2) * 2 + k // 2], index) for k in range(4)]
            moved = jnp.where(
                (lane32 // 8) % 2 == 0,
                jnp.where((lane32 // 4) % 2 == 0, four[0], four[1]),
                jnp.where((lane32 // 4) % 2 == 0, four[2], four[3]),
            )
            at = (slice(32 * v, 32 * v + 32), slice(SUB * j, SUB * (j + 1)))
            base_s[at] = spec_v[at] - (learn_rate * decay_rate) * moved

    arrived(zrb, NZ - 1, 7)
    agb[c, xy] = jnp.sum(zrb[...], axis=0)

    def send_gather(i, carry):
        send(agb.at[c, xy], agb.at[c, xy], 8, xy_peer(i)[1]).start()
        return carry

    lax.fori_loop(1, NXY, send_gather, 0, unroll=True)
    arrived(agb.at[c], NXY - 1, 8)
    send(agb.at[c], agb.at[c], 9, partner).start()
    send(agb.at[1 - c], agb.at[1 - c], 9, partner).wait_recv()
    total = jnp.concatenate([agb[h, p] for h in range(2) for p in range(NXY)], axis=0)

    lane = iota((WIDTH, SUB), 1)
    gain_back = jnp.zeros((WIDTH, SUB), F32)
    bias_back = jnp.zeros((WIDTH, SUB), F32)
    for j in range(16):
        cols = slice(SUB * j, SUB * (j + 1))
        index = jnp.where(lane < 64, 2 * j, 2 * j + 1)
        by_gain = take_lanes(total, index + LANE_P)
        by_bias = take_lanes(total, index + LANE_Q)
        grad = gain_lanes * by_gain + bias_lanes * by_bias
        grad_s[:, cols] = grad
        spec_o[:, cols] = base_s[:, cols] - learn_rate * grad
        w = spec_v[:, cols]
        gain_back = gain_back + by_gain * w
        bias_back = bias_back + by_bias * w

    dm1, dm0 = total[:, LANE_M1 : LANE_M1 + 1], total[:, LANE_M0 : LANE_M0 + 1]

    def to_column(back, dm):
        both = jnp.sum(back, axis=0, keepdims=True)
        both = both[:, 0:WIDTH] + both[:, WIDTH:] + jnp.sum(mixing * dm, axis=0, keepdims=True)
        return jnp.sum(jnp.where(eye, both, 0.0), axis=1, keepdims=True)

    dense_o[:, 0:64] = mixing - dense_rate * (gain_row * dm1 + bias_row * dm0)
    dense_o[:, 64:65] = dv[:, 64:65] - dense_rate * to_column(gain_back, dm1)
    dense_o[:, 65:66] = dv[:, 65:66] - dense_rate * to_column(bias_back, dm0)
    dense_o[:, 66:67] = layer_bias - dense_rate * dm0
    dense_o[:, 67:68] = proj - dense_rate * total[:, LANE_PROJ : LANE_PROJ + 1]

    mine = grad_s[:, pl.ds(pl.multiple_of((d // 32) * SUB, SUB), SUB)]
    mine = pltpu.roll(mine, lax.rem(SUB - lax.rem(d, 32) * 4, SUB), axis=1)
    mom_o[...] = decay_rate * mz[z] + mine.T[0:4, :]

    own = jnp.logical_and(iota((NS, SUB), 0) == s, lane == LANE_LOSS + g)
    own = jnp.sum(jnp.where(own, total, 0.0), axis=1, keepdims=True)
    loss_o[...] = jnp.sum(own, axis=0, keepdims=True)

    sent(edge_snd.at[0], 4, 0)
    sent(edge_snd.at[1], 4, 1)
    sent(mz, NZ - 1, 2)
    sent(gath.at[c], NXY - 1, 3)
    send(pay.at[1 - c], crs, 4, partner).wait_send()
    send(gath.at[c], gath.at[c], 5, partner).wait_send()
    sent(half_s, NXY - 1, 6)
    sent(zrb, NZ - 1, 7)
    sent(agb.at[c], NXY - 1, 8)
    send(agb.at[c], agb.at[c], 9, partner).wait_send()


def write(*refs):
    sources, results, sems = refs[:5], refs[5:10], refs[10]
    copies = [pltpu.make_async_copy(a, b, sems.at[i]) for i, (a, b) in enumerate(zip(sources, results))]
    for copy in copies:
        copy.start()
    for copy in copies:
        copy.wait()


def local(velocity, rate, forcing, anchor_line, anchor_z, assign, spectral, dense, momentum):
    smem = pl.BlockSpec(memory_space=pltpu.SMEM)
    hbm = pl.BlockSpec(memory_space=pltpu.HBM)
    whole = pl.BlockSpec(memory_space=pltpu.VMEM)
    vmem = pltpu.VMEM
    shapes = (
        jax.ShapeDtypeStruct((8, 8, 512), F32),
        jax.ShapeDtypeStruct((1, 1), F32),
        jax.ShapeDtypeStruct((WIDTH, 2048), F32),
        jax.ShapeDtypeStruct((WIDTH, 68), F32),
        jax.ShapeDtypeStruct((4, WIDTH), F32),
    )

    def pin(x):
        return pltpu.with_memory_space_constraint(x, pltpu.HBM)

    velocity, rate, forcing, momentum = pin(velocity), pin(rate), pin(forcing), pin(momentum)
    anchor_line, anchor_z = pin(anchor_line), pin(anchor_z)
    results = pl.pallas_call(
        kernel,
        out_shape=shapes,
        in_specs=[hbm, hbm, hbm, smem, smem, hbm, hbm, hbm, hbm, hbm],
        out_specs=(whole,) * 5,
        scratch_shapes=[
            vmem((8, 8, 512), F32),
            vmem((8, 8, 512), F32),
            vmem((8, 8, 512), F32),
            vmem((1, LINES), jnp.int32),
            vmem((WIDTH, 2048), F32),
            vmem((WIDTH, 68), F32),
            vmem((96, SUB), F32),
            vmem((2, 4, 8, 512), F32),
            vmem((2, 4, 8, 512), F32),
            vmem((64, 512), F32),
            vmem((64, 512), F32),
            vmem((2 * LINES, 512), F32),
            vmem((LINES, SUB), F32),
            vmem((3 * KEEP, 2048), BF16),
            vmem((2 * WIDTH, 2048), BF16),
            vmem((NZ, 4, WIDTH), F32),
            vmem((2, NXY, 32, SUB), F32),
            vmem((WIDTH, 2048), F32),
            vmem((WIDTH, 2048), F32),
            vmem((2, NXY, 2, SUB), F32),
            vmem((NXY, 2, SUB), F32),
            vmem((NXY, 2, SUB), F32),
            vmem((NXY, 2, SUB), F32),
            vmem((NZ, 2, SUB), F32),
            vmem((2, NXY, 2, SUB), F32),
            pltpu.SemaphoreType.DMA((8,)),
            pltpu.SemaphoreType.DMA((10,)),
            pltpu.SemaphoreType.DMA((10,)),
        ],
        compiler_params=pltpu.CompilerParams(
            collective_id=0, has_side_effects=True, vmem_limit_bytes=32 * 1024 * 1024
        ),
    )(velocity, rate, forcing, anchor_line, anchor_z, pin(assign.T), pin(spectral.T), pin(dense.T), momentum, pin(jnp.asarray(tables())))
    field, loss, spec, dens, mom = pl.pallas_call(
        write,
        out_shape=shapes,
        in_specs=[pl.BlockSpec(memory_space=pl.ANY)] * 5,
        out_specs=(hbm,) * 5,
        scratch_shapes=[pltpu.SemaphoreType.DMA((5,))],
        compiler_params=pltpu.CompilerParams(vmem_limit_bytes=1024 * 1024),
    )(*results)
    return (field, loss, spec.T, dens.T, mom)


def solution(mesh):
    placed = (
        P("grp", "slab", None),
        P("grp", "slab", None),
        P("grp", "slab", None),
        P(("grp", "slab")),
        P(("grp", "slab")),
        P(("grp", "slab"), None),
        P(),
        P(),
        P(("grp", "slab"), None),
    )
    return jax.shard_map(
        local,
        mesh=mesh,
        in_specs=placed,
        out_specs=(P("grp", "slab", None), P("grp", "slab"), P(), P(), P(("grp", "slab"), None)),
        check_vma=False,
    )
```

time: 62.3 us -> 53.5 us (0.86)
  local copies, waits for them, and re-layouts: 8.63 us -> 0 us
  between operations: 2.45 us -> 0.64 us
  Pallas kernels: 50.9 us -> 52.7 us
    unnamed x24 -> x0, local copies, waits for them, and re-layouts: 8.63 us -> none
    pallas_call x1 -> x2, Pallas kernels: 50.9 us -> 52.7 us  [the longest x1 51.2 us: local(): pl.pallas_call(kernel, out_shape=shapes, in_specs=[hbm, hbm, hbm, smem, s...]
where the time goes in v2:
time: 53.5 us; the launch traced here: 53.4 us
  Pallas kernels  52.7 us (99%)
  between operations  0.64 us (1%)
    pallas_call x1, Pallas kernels, local(): pl.pallas_call(kernel, out_shape=shapes, in_specs=[hbm, hbm, hbm, smem, s...  51.2 us
    pallas_call x1, Pallas kernels, local(): pl.pallas_call(write, out_shape=shapes, in_specs=[pl.BlockSpec(memory_spa...  1.52 us

profile of v2, /device:TPU:1, one launch (start us, length us, event | category | flops | bytes accessed | tf_op | source)
XLA Modules:
  0.0 53.4 jit_solution(13851484006831944670)
XLA Ops:
  0.6 51.2 %shard_map.137 = (f32[8,8,512]{2,1,0:T(8,128)S(1)}, f32[1,1]{1,0:T(1,128)}, f32[64,2048]{1,0:T(8,128)S(1)}, f32[64,68]{1,0:T(8,128)S(1)}, f32[4,64]{1,0:T(4,128)S(1)}) custom-call(f32[8,8,512]{2,1,0:T(8,128)} %vel.1, f32[8,8,512]{2,1,0:T(8,128)} %rate.1, f32[8,8,512]{2,1,0:T(8,128)} %forc.1, s32[16]{0:T(128)} %aline.1, s32[16]{0:T(128)} %az.1, ...), custom_call_target="tpu_custom_call" | custom-call | tf_op jit(solution)/shard_map/pallas_call | solution.py:451
  51.9 1.5 %shard_map.138 = (f32[8,8,512]{2,1,0:T(8,128)}, f32[1,1]{1,0:T(1,128)}, f32[64,2048]{1,0:T(8,128)}, f32[64,68]{1,0:T(8,128)}, f32[4,64]{1,0:T(4,128)}) custom-call(f32[8,8,512]{2,1,0:T(8,128)S(1)} %get-tuple-element.15.refs_0_, f32[1,1]{1,0:T(1,128)} %get-tuple-element.16.refs_1_, f32[64,2048]{1,0:T(8,128)S(1)} %get-tuple-element.17.refs_2_, ...), custom_call_target="tpu_custom_call" | custom-call | tf_op jit(solution)/shard_map/pallas_call | solution.py:490

commit v3 on v2

--- a/solution.py
+++ b/solution.py
@@ -25,6 +25,17 @@
 BF16 = jnp.bfloat16
 HIGHEST = lax.Precision.HIGHEST
 GELU_C = float(np.sqrt(2.0 / np.pi))
+
+Z_ORDER = (8, 7, 9, 6, 10, 5, 11, 4, 12, 3, 13, 2, 14, 1, 15)
+Z_NEAR = (3, 13, 2, 14, 1, 15)
+XY_ORDER = tuple(
+    sorted(
+        ((a, b, c) for a in range(2) for b in range(4) for c in range(2) if a + b + c),
+        key=lambda i: -(min(i[1], 4 - i[1]) + (2 * i[2] if not i[0] else 1)),
+    )
+)
+XY_ROW = ((1, 0, 0), (0, 0, 1), (1, 0, 1))
+XY_COLUMN = ((0, 1, 0), (0, 2, 0), (0, 3, 0))
 
 LANE_P = 0
 LANE_Q = 32
@@ -78,11 +89,11 @@
     vel, rate, forc, aline, az, assign, spec, dense, mom, tab,
     field_o, loss_o, spec_o, dense_o, mom_o,
     vel_v, rate_v, forc_v, asg_v, spec_v, dense_v, tab_v,
-    edge_snd, edge_rcv,
+    side_snd, side_rcv, corn_snd, corn_rcv,
     v1_s, chg_s, samp, diff_s, right, dp_s,
     mz, gath, base_s, grad_s,
     pay, crs, half_s, rsb, zrb, agb,
-    ld, ssem, rsem,
+    ld, ssem, rsem, know,
 ):
     g = lax.axis_index("grp")
     s = lax.axis_index("slab")
@@ -98,43 +109,34 @@
     def greet(device):
         pl.semaphore_signal(barrier, inc=1, device_id=device, device_id_type=MESH)
 
+    xl, y = g // 4, lax.rem(g, 4)
+
     def z_peer(i):
-        zz = lax.rem(z + i, NZ)
-        return (g, zz * 4 + xc)
+        return (g, lax.rem(z + i, NZ) * 4 + xc)
 
     def xy_peer(i):
-        p = lax.rem(xy + i, NXY)
-        return p, (p // 2, z * 4 + lax.rem(p, 2) * 2 + c)
-
-    sides = [
-        (lax.rem(g + 1, NG), s),
-        (lax.rem(g + NG - 1, NG), s),
-        (g, lax.rem(s + 1, NS)),
-        (g, lax.rem(s + NS - 1, NS)),
-    ]
+        flip_l, step, flip_h = i
+        gg = (xl + flip_l - 2 * flip_l * xl) * 4 + lax.rem(y + step, 4)
+        hh = xh + flip_h - 2 * flip_h * xh
+        return gg * 2 + hh, (gg, z * 4 + hh * 2 + c)
+
+    up_g, dn_g = lax.rem(g + 1, NG), lax.rem(g + NG - 1, NG)
+    up_s, dn_s = lax.rem(s + 1, NS), lax.rem(s + NS - 1, NS)
+    sides = [(up_g, s), (dn_g, s), (g, up_s), (g, dn_s)]
+    corners = [(up_g, up_s), (up_g, dn_s), (dn_g, up_s), (dn_g, dn_s)]
     partner = (g, s + 1 - 2 * c)
+
+    near = corners + [z_peer(i) for i in Z_NEAR] + [xy_peer(i)[1] for i in XY_ROW + XY_COLUMN] + sides + [partner]
 
     def load(src, dst, n):
         copy = pltpu.make_async_copy(src, dst, ld.at[n])
         copy.start()
         return copy
 
-    def greet_z(i, carry):
-        greet(z_peer(i))
-        return carry
-
-    def greet_xy(i, carry):
-        greet(xy_peer(i)[1])
-        return carry
-
-    vel_load = load(vel, vel_v, 0)
-    for device in sides:
+    flow_loads = [load(vel, vel_v, 0), load(rate, rate_v, 2), load(forc, forc_v, 3)]
+    for device in near:
         greet(device)
-    greet(partner)
-    lax.fori_loop(1, NZ, greet_z, 0, unroll=True)
-    lax.fori_loop(1, NXY, greet_xy, 0, unroll=True)
     mom_load = load(mom, mz.at[z], 1)
-    flow_loads = [load(rate, rate_v, 2), load(forc, forc_v, 3)]
     other_loads = [load(spec, spec_v, 4), load(dense, dense_v, 5), load(tab, tab_v, 6), load(assign, asg_v, 7)]
 
     def send(src, dst, n, device):
@@ -148,25 +150,39 @@
     def sent(buf, count, n):
         send(buf.at[pl.ds(0, count)], buf.at[pl.ds(0, count)], n, partner).wait_send()
 
-    def send_edges(phase):
-        for n in range(4):
-            send(edge_snd.at[phase, n], edge_rcv.at[phase, n], phase, sides[n]).start()
-
-    vel_load.wait()
-    edge_snd[0, 0] = vel_v[7]
-    edge_snd[0, 1] = vel_v[0]
-    edge_snd[0, 2] = vel_v[:, 7, :]
-    edge_snd[0, 3] = vel_v[:, 0, :]
-    pl.semaphore_wait(barrier, 5 + NZ - 1 + NXY - 1)
-    send_edges(0)
-
-    mom_load.wait()
-
-    def send_z(i, carry):
-        send(mz.at[z], mz.at[z], 2, z_peer(i)).start()
-        return carry
-
-    lax.fori_loop(1, NZ, send_z, 0, unroll=True)
+    def tell(n, device):
+        pl.semaphore_signal(know.at[n], inc=1, device_id=device, device_id_type=MESH)
+
+    row = iota((8, 512), 0)
+
+    def shifted(plane, before, after):
+        lo = jnp.where(row == 0, before, pltpu.roll(plane, 1, axis=0))
+        hi = jnp.where(row == 7, after, pltpu.roll(plane, 7, axis=0))
+        return lo + hi
+
+    def along(plane):
+        return pltpu.roll(plane, 1, axis=1) + pltpu.roll(plane, 511, axis=1)
+
+    for copy in flow_loads:
+        copy.wait()
+    for n, (a, b) in enumerate([(7, 6), (0, 1), (7, 6), (0, 1)]):
+        pick = (lambda ref, i: ref[i]) if n < 2 else (lambda ref, i: ref[:, i, :])
+        mid, far, r, f = pick(vel_v, a), pick(vel_v, b), pick(rate_v, a), pick(forc_v, a)
+        side_snd[n, 0] = mid
+        side_snd[n, 1] = mid + (r * (far + shifted(mid, 0.0, 0.0) + along(mid) - 6.0 * mid) + f)
+        side_snd[n, 2] = r
+    for n, (a, b) in enumerate([(7, 7), (7, 0), (0, 7), (0, 0)]):
+        corn_snd[n] = vel_v[a, b : b + 1, :]
+    pl.semaphore_wait(barrier, len(near))
+    for n in range(4):
+        send(side_snd.at[n], side_rcv.at[n], 0, sides[n]).start()
+    for n in range(4):
+        send(corn_snd.at[n], corn_rcv.at[n], 1, corners[n]).start()
+
+    for i in (3, NZ - 3):
+        tell(0, z_peer(i))
+    for i in XY_COLUMN:
+        tell(2, xy_peer(i)[1])
 
     for copy in other_loads:
         copy.wait()
@@ -201,45 +217,42 @@
         for t in range(LINES):
             right[row0 : row0 + 32, SUB * t : SUB * (t + 1)] = part
 
+    pl.semaphore_wait(know.at[0], 2)
+    for i in (2, NZ - 2):
+        tell(1, z_peer(i))
+
+    send(side_snd, side_rcv, 0, partner).wait_recv()
+    send(corn_snd, corn_rcv, 1, partner).wait_recv()
     has = [g > 0, g < NG - 1, s > 0, s < NS - 1]
-    row = iota((8, 512), 0)
-
-    def flow(cells, phase):
-        edge = [jnp.where(has[n], edge_rcv[phase, n], 0.0) for n in range(4)]
+    corner = [
+        jnp.where(jnp.logical_and(has[a], has[b]), corn_rcv[n], 0.0)
+        for n, (a, b) in enumerate([(0, 2), (0, 3), (1, 2), (1, 3)])
+    ]
+    edge0, edge1 = [], []
+    for n, (a, lo, hi) in enumerate([(0, 0, 1), (7, 2, 3), (0, 0, 2), (7, 1, 3)]):
+        mid, part, r = [jnp.where(has[n], side_rcv[n, i], 0.0) for i in range(3)]
+        own = vel_v[a] if n < 2 else vel_v[:, a, :]
+        ends = jnp.where(row == 0, corner[lo], jnp.where(row == 7, corner[hi], 0.0))
+        edge0.append(mid)
+        edge1.append(part + r * (own + ends))
+
+    def flow(cells, edge):
         changes = []
         for x in range(8):
             mid = cells[x]
             below = edge[0] if x == 0 else cells[x - 1]
             above = edge[1] if x == 7 else cells[x + 1]
-            left_of = jnp.where(row == 0, edge[2][x : x + 1, :], pltpu.roll(mid, 1, axis=0))
-            right_of = jnp.where(row == 7, edge[3][x : x + 1, :], pltpu.roll(mid, 7, axis=0))
-            beside = above + below + right_of + left_of
-            beside = beside + pltpu.roll(mid, 1, axis=1) + pltpu.roll(mid, 511, axis=1)
+            beside = above + below + shifted(mid, edge[2][x : x + 1, :], edge[3][x : x + 1, :]) + along(mid)
             changes.append(rate_v[x] * (beside - 6.0 * mid) + forc_v[x])
         return changes
 
-    for copy in flow_loads:
-        copy.wait()
-    arrived(edge_rcv.at[0], 4, 0)
     first = [vel_v[x] for x in range(8)]
-    second = [mid + change for mid, change in zip(first, flow(first, 0))]
-    edge_snd[1, 0] = second[7]
-    edge_snd[1, 1] = second[0]
-    edge_snd[1, 2] = jnp.concatenate([p[7:8, :] for p in second], axis=0)
-    edge_snd[1, 3] = jnp.concatenate([p[0:1, :] for p in second], axis=0)
-    send_edges(1)
+    second = [mid + change for mid, change in zip(first, flow(first, edge0))]
     for x in range(8):
         v1_s[8 * x : 8 * x + 8, :] = second[x]
-
-    arrived(mz, NZ - 1, 2)
-    turned = jnp.concatenate([mz[i] for i in range(NZ)], axis=0).T
-    gath[c, xy] = jnp.concatenate([turned[0:32, :], turned[32:64, :]], axis=1)
-
-    def send_xy(i, carry):
-        send(gath.at[c, xy], gath.at[c, xy], 3, xy_peer(i)[1]).start()
-        return carry
-
-    lax.fori_loop(1, NXY, send_xy, 0, unroll=True)
+    for x, change in enumerate(flow(second, edge1)):
+        chg_s[8 * x : 8 * x + 8, :] = change
+        field_o[x] = second[x] + change
 
     for t in range(LINES):
         samp[t : t + 1, :] = v1_s[pl.ds(aline[t], 1), :]
@@ -275,10 +288,6 @@
         right[144:160, one] = low
         right[224:240, one] = high
 
-    arrived(edge_rcv.at[1], 4, 1)
-    for x, change in enumerate(flow(second, 1)):
-        chg_s[8 * x : 8 * x + 8, :] = change
-        field_o[x] = second[x] + change
     for t in range(LINES):
         samp[LINES + t : LINES + t + 1, :] = chg_s[pl.ds(aline[t], 1), :]
     targets = jnp.concatenate([windows(2), windows(3)], axis=0)
@@ -324,27 +333,41 @@
 
     send(pay.at[1 - c], crs, 4, partner).start()
 
-    arrived(gath.at[c], NXY - 1, 3)
-    send(gath.at[c], gath.at[c], 5, partner).start()
+    pl.semaphore_wait(know.at[1], 2)
+    pl.semaphore_wait(know.at[2], 3)
+    mom_load.wait()
+    for i in Z_ORDER:
+        send(mz.at[z], mz.at[z], 2, z_peer(i)).start()
 
     send(pay.at[1 - c], crs, 4, partner).wait_recv()
     half_s[...] = pay[c] + crs[...]
 
-    def send_scatter(i, carry):
+    for i in XY_ORDER:
         p, device = xy_peer(i)
         send(half_s.at[p], rsb.at[xy], 6, device).start()
-        return carry
-
-    lax.fori_loop(1, NXY, send_scatter, 0, unroll=True)
     rsb[xy] = half_s[xy]
     arrived(rsb, NXY - 1, 6)
     zrb[z] = jnp.sum(rsb[...], axis=0)
 
-    def send_line(i, carry):
+    for i in Z_ORDER:
         send(zrb.at[z], zrb.at[z], 7, z_peer(i)).start()
-        return carry
-
-    lax.fori_loop(1, NZ, send_line, 0, unroll=True)
+
+    arrived(mz, NZ - 1, 2)
+    turned = jnp.concatenate([mz[i] for i in range(NZ)], axis=0).T
+    gath[c, xy] = jnp.concatenate([turned[0:32, :], turned[32:64, :]], axis=1)
+    for i in XY_ORDER:
+        send(gath.at[c, xy], gath.at[c, xy], 3, xy_peer(i)[1]).start()
+
+    arrived(zrb, NZ - 1, 7)
+    agb[c, xy] = jnp.sum(zrb[...], axis=0)
+
+    for i in XY_ORDER:
+        send(agb.at[c, xy], agb.at[c, xy], 8, xy_peer(i)[1]).start()
+
+    arrived(gath.at[c], NXY - 1, 3)
+    send(gath.at[c], gath.at[c], 5, partner).start()
+    arrived(agb.at[c], NXY - 1, 8)
+    send(agb.at[c], agb.at[c], 9, partner).start()
 
     send(gath.at[1 - c], gath.at[1 - c], 5, partner).wait_recv()
     lane32 = iota((32, SUB), 1)
@@ -360,16 +383,6 @@
             at = (slice(32 * v, 32 * v + 32), slice(SUB * j, SUB * (j + 1)))
             base_s[at] = spec_v[at] - (learn_rate * decay_rate) * moved
 
-    arrived(zrb, NZ - 1, 7)
-    agb[c, xy] = jnp.sum(zrb[...], axis=0)
-
-    def send_gather(i, carry):
-        send(agb.at[c, xy], agb.at[c, xy], 8, xy_peer(i)[1]).start()
-        return carry
-
-    lax.fori_loop(1, NXY, send_gather, 0, unroll=True)
-    arrived(agb.at[c], NXY - 1, 8)
-    send(agb.at[c], agb.at[c], 9, partner).start()
     send(agb.at[1 - c], agb.at[1 - c], 9, partner).wait_recv()
     total = jnp.concatenate([agb[h, p] for h in range(2) for p in range(NXY)], axis=0)
 
@@ -409,8 +422,8 @@
     own = jnp.sum(jnp.where(own, total, 0.0), axis=1, keepdims=True)
     loss_o[...] = jnp.sum(own, axis=0, keepdims=True)
 
-    sent(edge_snd.at[0], 4, 0)
-    sent(edge_snd.at[1], 4, 1)
+    send(side_snd, side_rcv, 0, partner).wait_send()
+    send(corn_snd, corn_rcv, 1, partner).wait_send()
     sent(mz, NZ - 1, 2)
     sent(gath.at[c], NXY - 1, 3)
     send(pay.at[1 - c], crs, 4, partner).wait_send()
@@ -461,8 +474,10 @@
             vmem((WIDTH, 2048), F32),
             vmem((WIDTH, 68), F32),
             vmem((96, SUB), F32),
-            vmem((2, 4, 8, 512), F32),
-            vmem((2, 4, 8, 512), F32),
+            vmem((4, 3, 8, 512), F32),
+            vmem((4, 3, 8, 512), F32),
+            vmem((4, 1, 512), F32),
+            vmem((4, 1, 512), F32),
             vmem((64, 512), F32),
             vmem((64, 512), F32),
             vmem((2 * LINES, 512), F32),
@@ -482,6 +497,7 @@
             pltpu.SemaphoreType.DMA((8,)),
             pltpu.SemaphoreType.DMA((10,)),
             pltpu.SemaphoreType.DMA((10,)),
+            pltpu.SemaphoreType.REGULAR((3,)),
         ],
         compiler_params=pltpu.CompilerParams(
             collective_id=0, has_side_effects=True, vmem_limit_bytes=32 * 1024 * 1024

time: 53.5 us -> 44.5 us (0.83)
  Pallas kernels: 52.7 us -> 43.7 us
    pallas_call x1, Pallas kernels: 51.2 us -> 42.2 us  [local(): pl.pallas_call(kernel, out_shape=shapes, in_specs=[hbm, hbm, hbm, smem, s...]
where the time goes in v3:
time: 44.5 us; the launch traced here: 44.4 us
  Pallas kernels  43.7 us (98%)
  between operations  0.64 us (1%)
    pallas_call x1, Pallas kernels, local(): pl.pallas_call(kernel, out_shape=shapes, in_specs=[hbm, hbm, hbm, smem, s...  42.2 us
    pallas_call x1, Pallas kernels, local(): pl.pallas_call(write, out_shape=shapes, in_specs=[pl.BlockSpec(memory_spa...  1.52 us

profile of v3, /device:TPU:1, one launch (start us, length us, event | category | flops | bytes accessed | tf_op | source)
XLA Modules:
  0.0 44.4 jit_solution(3391231184511261116)
XLA Ops:
  0.6 42.2 %shard_map.137 = (f32[8,8,512]{2,1,0:T(8,128)S(1)}, f32[1,1]{1,0:T(1,128)}, f32[64,2048]{1,0:T(8,128)S(1)}, f32[64,68]{1,0:T(8,128)S(1)}, f32[4,64]{1,0:T(4,128)S(1)}) custom-call(f32[8,8,512]{2,1,0:T(8,128)} %vel.1, f32[8,8,512]{2,1,0:T(8,128)} %rate.1, f32[8,8,512]{2,1,0:T(8,128)} %forc.1, s32[16]{0:T(128)} %aline.1, s32[16]{0:T(128)} %az.1, ...), custom_call_target="tpu_custom_call" | custom-call | tf_op jit(solution)/shard_map/pallas_call | solution.py:464
  42.9 1.5 %shard_map.138 = (f32[8,8,512]{2,1,0:T(8,128)}, f32[1,1]{1,0:T(1,128)}, f32[64,2048]{1,0:T(8,128)}, f32[64,68]{1,0:T(8,128)}, f32[4,64]{1,0:T(4,128)}) custom-call(f32[8,8,512]{2,1,0:T(8,128)S(1)} %get-tuple-element.15.refs_0_, f32[1,1]{1,0:T(1,128)} %get-tuple-element.16.refs_1_, f32[64,2048]{1,0:T(8,128)S(1)} %get-tuple-element.17.refs_2_, ...), custom_call_target="tpu_custom_call" | custom-call | tf_op jit(solution)/shard_map/pallas_call | solution.py:506

commit v4 on v3

--- a/solution.py
+++ b/solution.py
@@ -34,6 +34,8 @@
         key=lambda i: -(min(i[1], 4 - i[1]) + (2 * i[2] if not i[0] else 1)),
     )
 )
+PLANE_ORDER = tuple(i + (other,) for i in XY_ORDER for other in (1, 0)) + ((0, 0, 0, 1),)
+PLANE_FAR = 14
 XY_ROW = ((1, 0, 0), (0, 0, 1), (1, 0, 1))
 XY_COLUMN = ((0, 1, 0), (0, 2, 0), (0, 3, 0))
 
@@ -86,13 +88,13 @@
 
 
 def kernel(
-    vel, rate, forc, aline, az, assign, spec, dense, mom, tab,
+    vel, rate, forc, aline_h, az_h, assign, spec, dense, mom, tab,
     field_o, loss_o, spec_o, dense_o, mom_o,
     vel_v, rate_v, forc_v, asg_v, spec_v, dense_v, tab_v,
     side_snd, side_rcv, corn_snd, corn_rcv,
     v1_s, chg_s, samp, diff_s, right, dp_s,
     mz, gath, base_s, grad_s,
-    pay, crs, half_s, rsb, zrb, agb,
+    pay, rsb, zrb, agb, aline, az,
     ld, ssem, rsem, know,
 ):
     g = lax.axis_index("grp")
@@ -120,6 +122,13 @@
         hh = xh + flip_h - 2 * flip_h * xh
         return gg * 2 + hh, (gg, z * 4 + hh * 2 + c)
 
+    me = c * NXY + xy
+
+    def plane_peer(i):
+        p, (gg, ss) = xy_peer(i[:3])
+        cc = c + i[3] - 2 * i[3] * c
+        return cc * NXY + p, (gg, ss + cc - c)
+
     up_g, dn_g = lax.rem(g + 1, NG), lax.rem(g + NG - 1, NG)
     up_s, dn_s = lax.rem(s + 1, NS), lax.rem(s + NS - 1, NS)
     sides = [(up_g, s), (dn_g, s), (g, up_s), (g, dn_s)]
@@ -138,6 +147,7 @@
         greet(device)
     mom_load = load(mom, mz.at[z], 1)
     other_loads = [load(spec, spec_v, 4), load(dense, dense_v, 5), load(tab, tab_v, 6), load(assign, asg_v, 7)]
+    other_loads += [load(aline_h, aline, 8), load(az_h, az, 9)]
 
     def send(src, dst, n, device):
         return pltpu.make_async_remote_copy(
@@ -217,6 +227,8 @@
         for t in range(LINES):
             right[row0 : row0 + 32, SUB * t : SUB * (t + 1)] = part
 
+    pl.semaphore_wait(know.at[2], 3)
+    tell(3, partner)
     pl.semaphore_wait(know.at[0], 2)
     for i in (2, NZ - 2):
         tell(1, z_peer(i))
@@ -327,26 +339,25 @@
     grads = jnp.where(keep == LANE_PROJ, jnp.sum(proj_grad, axis=1, keepdims=True), grads)
     grads = jnp.where(keep == LANE_LOSS + g, loss, grads)
     payload = jnp.concatenate([grads, jnp.zeros((WIDTH, SUB - KEEP), F32)], axis=1)
-    for h in range(2):
-        for p in range(NXY):
-            pay[h, p] = payload[32 * h + 2 * p : 32 * h + 2 * p + 2, :]
-
-    send(pay.at[1 - c], crs, 4, partner).start()
+    for p in range(2 * NXY):
+        pay[p] = payload[2 * p : 2 * p + 2, :]
+
+    def scatter(order):
+        for i in order:
+            p, device = plane_peer(i)
+            send(pay.at[p], rsb.at[me], 6, device).start()
+
+    pl.semaphore_wait(know.at[3], 1)
+    scatter(PLANE_ORDER[:PLANE_FAR])
 
     pl.semaphore_wait(know.at[1], 2)
-    pl.semaphore_wait(know.at[2], 3)
     mom_load.wait()
     for i in Z_ORDER:
         send(mz.at[z], mz.at[z], 2, z_peer(i)).start()
 
-    send(pay.at[1 - c], crs, 4, partner).wait_recv()
-    half_s[...] = pay[c] + crs[...]
-
-    for i in XY_ORDER:
-        p, device = xy_peer(i)
-        send(half_s.at[p], rsb.at[xy], 6, device).start()
-    rsb[xy] = half_s[xy]
-    arrived(rsb, NXY - 1, 6)
+    scatter(PLANE_ORDER[PLANE_FAR:])
+    rsb[me] = pay[me]
+    arrived(rsb, 2 * NXY - 1, 6)
     zrb[z] = jnp.sum(rsb[...], axis=0)
 
     for i in Z_ORDER:
@@ -359,32 +370,29 @@
         send(gath.at[c, xy], gath.at[c, xy], 3, xy_peer(i)[1]).start()
 
     arrived(zrb, NZ - 1, 7)
-    agb[c, xy] = jnp.sum(zrb[...], axis=0)
-
-    for i in XY_ORDER:
-        send(agb.at[c, xy], agb.at[c, xy], 8, xy_peer(i)[1]).start()
+    agb[me] = jnp.sum(zrb[...], axis=0)
+    for i in PLANE_ORDER:
+        send(agb.at[me], agb.at[me], 4, plane_peer(i)[1]).start()
 
     arrived(gath.at[c], NXY - 1, 3)
     send(gath.at[c], gath.at[c], 5, partner).start()
-    arrived(agb.at[c], NXY - 1, 8)
-    send(agb.at[c], agb.at[c], 9, partner).start()
-
+    lane32 = iota((32, SUB), 1)
+
+    def unpack(share, before):
+        for j in range(16):
+            for v in range(2):
+                index = v * 64 + ((j % 2) * 8 + lane32 // 16) * 4 + lane32 % 4
+                two = [take_lanes(gath[share, (j // 2) * 2 + h], index) for h in range(2)]
+                moved = jnp.where((lane32 // 8) % 2 == 0, two[0], two[1])
+                moved = jnp.where((lane32 // 4) % 2 == share, moved, 0.0)
+                at = (slice(32 * v, 32 * v + 32), slice(SUB * j, SUB * (j + 1)))
+                base_s[at] = before[at] - (learn_rate * decay_rate) * moved
+
+    unpack(c, spec_v)
     send(gath.at[1 - c], gath.at[1 - c], 5, partner).wait_recv()
-    lane32 = iota((32, SUB), 1)
-    for j in range(16):
-        for v in range(2):
-            index = v * 64 + ((j % 2) * 8 + lane32 // 16) * 4 + lane32 % 4
-            four = [take_lanes(gath[k % 2, (j // 2) * 2 + k // 2], index) for k in range(4)]
-            moved = jnp.where(
-                (lane32 // 8) % 2 == 0,
-                jnp.where((lane32 // 4) % 2 == 0, four[0], four[1]),
-                jnp.where((lane32 // 4) % 2 == 0, four[2], four[3]),
-            )
-            at = (slice(32 * v, 32 * v + 32), slice(SUB * j, SUB * (j + 1)))
-            base_s[at] = spec_v[at] - (learn_rate * decay_rate) * moved
-
-    send(agb.at[1 - c], agb.at[1 - c], 9, partner).wait_recv()
-    total = jnp.concatenate([agb[h, p] for h in range(2) for p in range(NXY)], axis=0)
+    unpack(1 - c, base_s)
+    arrived(agb, 2 * NXY - 1, 4)
+    total = jnp.concatenate([agb[p] for p in range(2 * NXY)], axis=0)
 
     lane = iota((WIDTH, SUB), 1)
     gain_back = jnp.zeros((WIDTH, SUB), F32)
@@ -426,12 +434,10 @@
     send(corn_snd, corn_rcv, 1, partner).wait_send()
     sent(mz, NZ - 1, 2)
     sent(gath.at[c], NXY - 1, 3)
-    send(pay.at[1 - c], crs, 4, partner).wait_send()
     send(gath.at[c], gath.at[c], 5, partner).wait_send()
-    sent(half_s, NXY - 1, 6)
+    sent(pay, 2 * NXY - 1, 6)
     sent(zrb, NZ - 1, 7)
-    sent(agb.at[c], NXY - 1, 8)
-    send(agb.at[c], agb.at[c], 9, partner).wait_send()
+    sent(agb, 2 * NXY - 1, 4)
 
 
 def write(*refs):
@@ -444,7 +450,6 @@
 
 
 def local(velocity, rate, forcing, anchor_line, anchor_z, assign, spectral, dense, momentum):
-    smem = pl.BlockSpec(memory_space=pltpu.SMEM)
     hbm = pl.BlockSpec(memory_space=pltpu.HBM)
     whole = pl.BlockSpec(memory_space=pltpu.VMEM)
     vmem = pltpu.VMEM
@@ -464,7 +469,7 @@
     results = pl.pallas_call(
         kernel,
         out_shape=shapes,
-        in_specs=[hbm, hbm, hbm, smem, smem, hbm, hbm, hbm, hbm, hbm],
+        in_specs=[hbm] * 10,
         out_specs=(whole,) * 5,
         scratch_shapes=[
             vmem((8, 8, 512), F32),
@@ -488,16 +493,16 @@
             vmem((2, NXY, 32, SUB), F32),
             vmem((WIDTH, 2048), F32),
             vmem((WIDTH, 2048), F32),
-            vmem((2, NXY, 2, SUB), F32),
-            vmem((NXY, 2, SUB), F32),
-            vmem((NXY, 2, SUB), F32),
-            vmem((NXY, 2, SUB), F32),
+            vmem((2 * NXY, 2, SUB), F32),
+            vmem((2 * NXY, 2, SUB), F32),
             vmem((NZ, 2, SUB), F32),
-            vmem((2, NXY, 2, SUB), F32),
+            vmem((2 * NXY, 2, SUB), F32),
+            pltpu.SMEM((LINES,), jnp.int32),
+            pltpu.SMEM((LINES,), jnp.int32),
+            pltpu.SemaphoreType.DMA((10,)),
             pltpu.SemaphoreType.DMA((8,)),
-            pltpu.SemaphoreType.DMA((10,)),
-            pltpu.SemaphoreType.DMA((10,)),
-            pltpu.SemaphoreType.REGULAR((3,)),
+            pltpu.SemaphoreType.DMA((8,)),
+            pltpu.SemaphoreType.REGULAR((4,)),
         ],
         compiler_params=pltpu.CompilerParams(
             collective_id=0, has_side_effects=True, vmem_limit_bytes=32 * 1024 * 1024

time: 44.5 us -> 42.1 us (0.946)
  Pallas kernels: 43.7 us -> 41.3 us
    pallas_call x1, Pallas kernels: 42.2 us -> 39.8 us  [local(): pl.pallas_call(kernel, out_shape=shapes, in_specs=[hbm] * 10, out_specs=(...]
where the time goes in v4:
time: 42.1 us; the launch traced here: 42 us
  Pallas kernels  41.3 us (98%)
  between operations  0.64 us (2%)
    pallas_call x1, Pallas kernels, local(): pl.pallas_call(kernel, out_shape=shapes, in_specs=[hbm] * 10, out_specs=(...  39.8 us
    pallas_call x1, Pallas kernels, local(): pl.pallas_call(write, out_shape=shapes, in_specs=[pl.BlockSpec(memory_spa...  1.52 us

profile of v4, /device:TPU:1, one launch (start us, length us, event | category | flops | bytes accessed | tf_op | source)
XLA Modules:
  0.0 42.0 jit_solution(14841398131014463086)
XLA Ops:
  0.6 39.8 %shard_map.137 = (f32[8,8,512]{2,1,0:T(8,128)S(1)}, f32[1,1]{1,0:T(1,128)}, f32[64,2048]{1,0:T(8,128)S(1)}, f32[64,68]{1,0:T(8,128)S(1)}, f32[4,64]{1,0:T(4,128)S(1)}) custom-call(f32[8,8,512]{2,1,0:T(8,128)} %vel.1, f32[8,8,512]{2,1,0:T(8,128)} %rate.1, f32[8,8,512]{2,1,0:T(8,128)} %forc.1, s32[16]{0:T(128)} %aline_h.1, s32[16]{0:T(128)} %az_h.1, ...), custom_call_target="tpu_custom_call" | custom-call | tf_op jit(solution)/shard_map/pallas_call | solution.py:469
  40.5 1.5 %shard_map.138 = (f32[8,8,512]{2,1,0:T(8,128)}, f32[1,1]{1,0:T(1,128)}, f32[64,2048]{1,0:T(8,128)}, f32[64,68]{1,0:T(8,128)}, f32[4,64]{1,0:T(4,128)}) custom-call(f32[8,8,512]{2,1,0:T(8,128)S(1)} %get-tuple-element.15.refs_0_, f32[1,1]{1,0:T(1,128)} %get-tuple-element.16.refs_1_, f32[64,2048]{1,0:T(8,128)S(1)} %get-tuple-element.17.refs_2_, ...), custom_call_target="tpu_custom_call" | custom-call | tf_op jit(solution)/shard_map/pallas_call | solution.py:511

commit v5 on v4

--- a/solution.py
+++ b/solution.py
@@ -27,7 +27,7 @@
 GELU_C = float(np.sqrt(2.0 / np.pi))
 
 Z_ORDER = (8, 7, 9, 6, 10, 5, 11, 4, 12, 3, 13, 2, 14, 1, 15)
-Z_NEAR = (3, 13, 2, 14, 1, 15)
+Z_NEAR = (4, 12, 3, 13, 2, 14, 1, 15)
 XY_ORDER = tuple(
     sorted(
         ((a, b, c) for a in range(2) for b in range(4) for c in range(2) if a + b + c),
@@ -35,7 +35,6 @@
     )
 )
 PLANE_ORDER = tuple(i + (other,) for i in XY_ORDER for other in (1, 0)) + ((0, 0, 0, 1),)
-PLANE_FAR = 14
 XY_ROW = ((1, 0, 0), (0, 0, 1), (1, 0, 1))
 XY_COLUMN = ((0, 1, 0), (0, 2, 0), (0, 3, 0))
 
@@ -189,10 +188,10 @@
     for n in range(4):
         send(corn_snd.at[n], corn_rcv.at[n], 1, corners[n]).start()
 
-    for i in (3, NZ - 3):
+    for i in (4, NZ - 4):
         tell(0, z_peer(i))
     for i in XY_COLUMN:
-        tell(2, xy_peer(i)[1])
+        tell(1, xy_peer(i)[1])
 
     for copy in other_loads:
         copy.wait()
@@ -227,26 +226,16 @@
         for t in range(LINES):
             right[row0 : row0 + 32, SUB * t : SUB * (t + 1)] = part
 
-    pl.semaphore_wait(know.at[2], 3)
-    tell(3, partner)
+    pl.semaphore_wait(know.at[1], 3)
+    tell(2, partner)
     pl.semaphore_wait(know.at[0], 2)
-    for i in (2, NZ - 2):
-        tell(1, z_peer(i))
+    mom_load.wait()
+    for i in Z_ORDER:
+        send(mz.at[z], mz.at[z], 2, z_peer(i)).start()
 
     send(side_snd, side_rcv, 0, partner).wait_recv()
-    send(corn_snd, corn_rcv, 1, partner).wait_recv()
     has = [g > 0, g < NG - 1, s > 0, s < NS - 1]
-    corner = [
-        jnp.where(jnp.logical_and(has[a], has[b]), corn_rcv[n], 0.0)
-        for n, (a, b) in enumerate([(0, 2), (0, 3), (1, 2), (1, 3)])
-    ]
-    edge0, edge1 = [], []
-    for n, (a, lo, hi) in enumerate([(0, 0, 1), (7, 2, 3), (0, 0, 2), (7, 1, 3)]):
-        mid, part, r = [jnp.where(has[n], side_rcv[n, i], 0.0) for i in range(3)]
-        own = vel_v[a] if n < 2 else vel_v[:, a, :]
-        ends = jnp.where(row == 0, corner[lo], jnp.where(row == 7, corner[hi], 0.0))
-        edge0.append(mid)
-        edge1.append(part + r * (own + ends))
+    edge0 = [jnp.where(has[n], side_rcv[n, 0], 0.0) for n in range(4)]
 
     def flow(cells, edge):
         changes = []
@@ -262,10 +251,6 @@
     second = [mid + change for mid, change in zip(first, flow(first, edge0))]
     for x in range(8):
         v1_s[8 * x : 8 * x + 8, :] = second[x]
-    for x, change in enumerate(flow(second, edge1)):
-        chg_s[8 * x : 8 * x + 8, :] = change
-        field_o[x] = second[x] + change
-
     for t in range(LINES):
         samp[t : t + 1, :] = v1_s[pl.ds(aline[t], 1), :]
     row8 = iota((8, SUB), 0)
@@ -300,6 +285,21 @@
         right[144:160, one] = low
         right[224:240, one] = high
 
+    send(corn_snd, corn_rcv, 1, partner).wait_recv()
+    corner = [
+        jnp.where(jnp.logical_and(has[a], has[b]), corn_rcv[n], 0.0)
+        for n, (a, b) in enumerate([(0, 2), (0, 3), (1, 2), (1, 3)])
+    ]
+    edge1 = []
+    for n, (a, lo, hi) in enumerate([(0, 0, 1), (7, 2, 3), (0, 0, 2), (7, 1, 3)]):
+        part, r = [jnp.where(has[n], side_rcv[n, i], 0.0) for i in (1, 2)]
+        own = vel_v[a] if n < 2 else vel_v[:, a, :]
+        ends = jnp.where(row == 0, corner[lo], jnp.where(row == 7, corner[hi], 0.0))
+        edge1.append(part + r * (own + ends))
+
+    for x, change in enumerate(flow(second, edge1)):
+        chg_s[8 * x : 8 * x + 8, :] = change
+        field_o[x] = second[x] + change
     for t in range(LINES):
         samp[LINES + t : LINES + t + 1, :] = chg_s[pl.ds(aline[t], 1), :]
     targets = jnp.concatenate([windows(2), windows(3)], axis=0)
@@ -347,15 +347,8 @@
             p, device = plane_peer(i)
             send(pay.at[p], rsb.at[me], 6, device).start()
 
-    pl.semaphore_wait(know.at[3], 1)
-    scatter(PLANE_ORDER[:PLANE_FAR])
-
-    pl.semaphore_wait(know.at[1], 2)
-    mom_load.wait()
-    for i in Z_ORDER:
-        send(mz.at[z], mz.at[z], 2, z_peer(i)).start()
-
-    scatter(PLANE_ORDER[PLANE_FAR:])
+    pl.semaphore_wait(know.at[2], 1)
+    scatter(PLANE_ORDER)
     rsb[me] = pay[me]
     arrived(rsb, 2 * NXY - 1, 6)
     zrb[z] = jnp.sum(rsb[...], axis=0)
@@ -442,7 +435,10 @@
 
 def write(*refs):
     sources, results, sems = refs[:5], refs[5:10], refs[10]
-    copies = [pltpu.make_async_copy(a, b, sems.at[i]) for i, (a, b) in enumerate(zip(sources, results))]
+    pairs = [(sources[2].at[pl.ds(16 * i, 16)], results[2].at[pl.ds(16 * i, 16)]) for i in range(4)]
+    pairs += [(sources[0].at[pl.ds(4 * i, 4)], results[0].at[pl.ds(4 * i, 4)]) for i in range(2)]
+    pairs += [(sources[i], results[i]) for i in (1, 3, 4)]
+    copies = [pltpu.make_async_copy(a, b, sems.at[i]) for i, (a, b) in enumerate(pairs)]
     for copy in copies:
         copy.start()
     for copy in copies:
@@ -502,7 +498,7 @@
             pltpu.SemaphoreType.DMA((10,)),
             pltpu.SemaphoreType.DMA((8,)),
             pltpu.SemaphoreType.DMA((8,)),
-            pltpu.SemaphoreType.REGULAR((4,)),
+            pltpu.SemaphoreType.REGULAR((3,)),
         ],
         compiler_params=pltpu.CompilerParams(
             collective_id=0, has_side_effects=True, vmem_limit_bytes=32 * 1024 * 1024
@@ -513,7 +509,7 @@
         out_shape=shapes,
         in_specs=[pl.BlockSpec(memory_space=pl.ANY)] * 5,
         out_specs=(hbm,) * 5,
-        scratch_shapes=[pltpu.SemaphoreType.DMA((5,))],
+        scratch_shapes=[pltpu.SemaphoreType.DMA((9,))],
         compiler_params=pltpu.CompilerParams(vmem_limit_bytes=1024 * 1024),
     )(*results)
     return (field, loss, spec.T, dens.T, mom)

time: 42.1 us -> 41.7 us (level)
    pallas_call x1, Pallas kernels: 39.8 us -> 39.4 us  [local(): pl.pallas_call(kernel, out_shape=shapes, in_specs=[hbm] * 10, out_specs=(...]
where the time goes in v5:
time: 41.7 us; the launch traced here: 41.6 us
  Pallas kernels  40.9 us (98%)
  between operations  0.64 us (2%)
    pallas_call x1, Pallas kernels, local(): pl.pallas_call(kernel, out_shape=shapes, in_specs=[hbm] * 10, out_specs=(...  39.4 us
    pallas_call x1, Pallas kernels, local(): pl.pallas_call(write, out_shape=shapes, in_specs=[pl.BlockSpec(memory_spa...  1.55 us

profile of v5, /device:TPU:1, one launch (start us, length us, event | category | flops | bytes accessed | tf_op | source)
XLA Modules:
  0.0 41.6 jit_solution(3577575533397495070)
XLA Ops:
  0.6 39.4 %shard_map.137 = (f32[8,8,512]{2,1,0:T(8,128)S(1)}, f32[1,1]{1,0:T(1,128)}, f32[64,2048]{1,0:T(8,128)S(1)}, f32[64,68]{1,0:T(8,128)S(1)}, f32[4,64]{1,0:T(4,128)S(1)}) custom-call(f32[8,8,512]{2,1,0:T(8,128)} %vel.1, f32[8,8,512]{2,1,0:T(8,128)} %rate.1, f32[8,8,512]{2,1,0:T(8,128)} %forc.1, s32[16]{0:T(128)} %aline_h.1, s32[16]{0:T(128)} %az_h.1, ...), custom_call_target="tpu_custom_call" | custom-call | tf_op jit(solution)/shard_map/pallas_call | solution.py:465
  40.0 1.5 %shard_map.138 = (f32[8,8,512]{2,1,0:T(8,128)}, f32[1,1]{1,0:T(1,128)}, f32[64,2048]{1,0:T(8,128)}, f32[64,68]{1,0:T(8,128)}, f32[4,64]{1,0:T(4,128)}) custom-call(f32[8,8,512]{2,1,0:T(8,128)S(1)} %get-tuple-element.15.refs_0_, f32[1,1]{1,0:T(1,128)} %get-tuple-element.16.refs_1_, f32[64,2048]{1,0:T(8,128)S(1)} %get-tuple-element.17.refs_2_, ...), custom_call_target="tpu_custom_call" | custom-call | tf_op jit(solution)/shard_map/pallas_call | solution.py:507

commit v6 on v5

--- a/solution.py
+++ b/solution.py
@@ -35,6 +35,7 @@
     )
 )
 PLANE_ORDER = tuple(i + (other,) for i in XY_ORDER for other in (1, 0)) + ((0, 0, 0, 1),)
+RING_ORDER = tuple(i for i in PLANE_ORDER if i[1] == 0)
 XY_ROW = ((1, 0, 0), (0, 0, 1), (1, 0, 1))
 XY_COLUMN = ((0, 1, 0), (0, 2, 0), (0, 3, 0))
 
@@ -122,11 +123,12 @@
         return gg * 2 + hh, (gg, z * 4 + hh * 2 + c)
 
     me = c * NXY + xy
+    piece = (xl * 2 + xh) * 2 + c
 
     def plane_peer(i):
         p, (gg, ss) = xy_peer(i[:3])
         cc = c + i[3] - 2 * i[3] * c
-        return cc * NXY + p, (gg, ss + cc - c)
+        return (p // 8 * 2 + lax.rem(p, 2)) * 2 + cc, (gg, ss + cc - c)
 
     up_g, dn_g = lax.rem(g + 1, NG), lax.rem(g + NG - 1, NG)
     up_s, dn_s = lax.rem(s + 1, NS), lax.rem(s + NS - 1, NS)
@@ -141,9 +143,9 @@
         copy.start()
         return copy
 
-    flow_loads = [load(vel, vel_v, 0), load(rate, rate_v, 2), load(forc, forc_v, 3)]
     for device in near:
         greet(device)
+    flow_loads = [load(vel, vel_v, 0), load(rate, rate_v, 2), load(forc, forc_v, 3)]
     mom_load = load(mom, mz.at[z], 1)
     other_loads = [load(spec, spec_v, 4), load(dense, dense_v, 5), load(tab, tab_v, 6), load(assign, asg_v, 7)]
     other_loads += [load(aline_h, aline, 8), load(az_h, az, 9)]
@@ -339,8 +341,8 @@
     grads = jnp.where(keep == LANE_PROJ, jnp.sum(proj_grad, axis=1, keepdims=True), grads)
     grads = jnp.where(keep == LANE_LOSS + g, loss, grads)
     payload = jnp.concatenate([grads, jnp.zeros((WIDTH, SUB - KEEP), F32)], axis=1)
-    for p in range(2 * NXY):
-        pay[p] = payload[2 * p : 2 * p + 2, :]
+    for p in range(8):
+        pay[p] = payload[8 * p : 8 * p + 8, :]
 
     def scatter(order):
         for i in order:
@@ -349,7 +351,7 @@
 
     pl.semaphore_wait(know.at[2], 1)
     scatter(PLANE_ORDER)
-    rsb[me] = pay[me]
+    rsb[me] = pay[piece]
     arrived(rsb, 2 * NXY - 1, 6)
     zrb[z] = jnp.sum(rsb[...], axis=0)
 
@@ -363,9 +365,9 @@
         send(gath.at[c, xy], gath.at[c, xy], 3, xy_peer(i)[1]).start()
 
     arrived(zrb, NZ - 1, 7)
-    agb[me] = jnp.sum(zrb[...], axis=0)
-    for i in PLANE_ORDER:
-        send(agb.at[me], agb.at[me], 4, plane_peer(i)[1]).start()
+    agb[piece] = jnp.sum(zrb[...], axis=0)
+    for i in RING_ORDER:
+        send(agb.at[piece], agb.at[piece], 4, plane_peer(i)[1]).start()
 
     arrived(gath.at[c], NXY - 1, 3)
     send(gath.at[c], gath.at[c], 5, partner).start()
@@ -384,8 +386,8 @@
     unpack(c, spec_v)
     send(gath.at[1 - c], gath.at[1 - c], 5, partner).wait_recv()
     unpack(1 - c, base_s)
-    arrived(agb, 2 * NXY - 1, 4)
-    total = jnp.concatenate([agb[p] for p in range(2 * NXY)], axis=0)
+    arrived(agb, 7, 4)
+    total = agb[...].reshape(WIDTH, SUB)
 
     lane = iota((WIDTH, SUB), 1)
     gain_back = jnp.zeros((WIDTH, SUB), F32)
@@ -428,9 +430,9 @@
     sent(mz, NZ - 1, 2)
     sent(gath.at[c], NXY - 1, 3)
     send(gath.at[c], gath.at[c], 5, partner).wait_send()
-    sent(pay, 2 * NXY - 1, 6)
+    sent(rsb, 2 * NXY - 1, 6)
     sent(zrb, NZ - 1, 7)
-    sent(agb, 2 * NXY - 1, 4)
+    sent(agb, 7, 4)
 
 
 def write(*refs):
@@ -489,10 +491,10 @@
             vmem((2, NXY, 32, SUB), F32),
             vmem((WIDTH, 2048), F32),
             vmem((WIDTH, 2048), F32),
-            vmem((2 * NXY, 2, SUB), F32),
-            vmem((2 * NXY, 2, SUB), F32),
-            vmem((NZ, 2, SUB), F32),
-            vmem((2 * NXY, 2, SUB), F32),
+            vmem((8, 8, SUB), F32),
+            vmem((2 * NXY, 8, SUB), F32),
+            vmem((NZ, 8, SUB), F32),
+            vmem((8, 8, SUB), F32),
             pltpu.SMEM((LINES,), jnp.int32),
             pltpu.SMEM((LINES,), jnp.int32),
             pltpu.SemaphoreType.DMA((10,)),

time: 41.7 us -> 40.9 us (0.981)
  Pallas kernels: 40.9 us -> 40.1 us
    pallas_call x1, Pallas kernels: 39.4 us -> 38.6 us  [local(): pl.pallas_call(kernel, out_shape=shapes, in_specs=[hbm] * 10, out_specs=(...]
where the time goes in v6:
time: 40.9 us; the launch traced here: 40.8 us
  Pallas kernels  40.1 us (98%)
  between operations  0.64 us (2%)
    pallas_call x1, Pallas kernels, local(): pl.pallas_call(kernel, out_shape=shapes, in_specs=[hbm] * 10, out_specs=(...  38.6 us
    pallas_call x1, Pallas kernels, local(): pl.pallas_call(write, out_shape=shapes, in_specs=[pl.BlockSpec(memory_spa...  1.55 us

profile of v6, /device:TPU:1, one launch (start us, length us, event | category | flops | bytes accessed | tf_op | source)
XLA Modules:
  0.0 40.8 jit_solution(17430408525998757158)
XLA Ops:
  0.6 38.6 %shard_map.137 = (f32[8,8,512]{2,1,0:T(8,128)S(1)}, f32[1,1]{1,0:T(1,128)}, f32[64,2048]{1,0:T(8,128)S(1)}, f32[64,68]{1,0:T(8,128)S(1)}, f32[4,64]{1,0:T(4,128)S(1)}) custom-call(f32[8,8,512]{2,1,0:T(8,128)} %vel.1, f32[8,8,512]{2,1,0:T(8,128)} %rate.1, f32[8,8,512]{2,1,0:T(8,128)} %forc.1, s32[16]{0:T(128)} %aline_h.1, s32[16]{0:T(128)} %az_h.1, ...), custom_call_target="tpu_custom_call" | custom-call | tf_op jit(solution)/shard_map/pallas_call | solution.py:467
  39.2 1.5 %shard_map.138 = (f32[8,8,512]{2,1,0:T(8,128)}, f32[1,1]{1,0:T(1,128)}, f32[64,2048]{1,0:T(8,128)}, f32[64,68]{1,0:T(8,128)}, f32[4,64]{1,0:T(4,128)}) custom-call(f32[8,8,512]{2,1,0:T(8,128)S(1)} %get-tuple-element.15.refs_0_, f32[1,1]{1,0:T(1,128)} %get-tuple-element.16.refs_1_, f32[64,2048]{1,0:T(8,128)S(1)} %get-tuple-element.17.refs_2_, ...), custom_call_target="tpu_custom_call" | custom-call | tf_op jit(solution)/shard_map/pallas_call | solution.py:509

commit v7 on v6

--- a/solution.py
+++ b/solution.py
@@ -23,7 +23,6 @@
 MESH = pl.DeviceIdType.MESH
 F32 = jnp.float32
 BF16 = jnp.bfloat16
-HIGHEST = lax.Precision.HIGHEST
 GELU_C = float(np.sqrt(2.0 / np.pi))
 
 Z_ORDER = (8, 7, 9, 6, 10, 5, 11, 4, 12, 3, 13, 2, 14, 1, 15)
@@ -60,8 +59,8 @@
     return np.concatenate([cos, -sin, weight * cos, weight * sin, a0, b0]).astype(np.float32)
 
 
-def nt(a, b, precision=None):
-    return lax.dot_general(a, b, (((1,), (1,)), ((), ())), precision=precision, preferred_element_type=F32)
+def nt(a, b):
+    return lax.dot_general(a, b, (((1,), (1,)), ((), ())), preferred_element_type=F32)
 
 
 def nn(a, b):
@@ -270,7 +269,8 @@
         return jnp.where(at < SUB, take_lanes(lo, index), take_lanes(hi, index))
 
     inputs = jnp.concatenate([windows(0), windows(1)], axis=0)
-    spectrum = nt(tab_v[0:32, :], inputs, HIGHEST)
+    waves_of = nt(jnp.concatenate(parts(tab_v[0:32, :]), axis=0), jnp.concatenate(parts(inputs), axis=0))
+    spectrum = waves_of[0:32, 0:LINES] + waves_of[0:32, LINES:] + waves_of[32:64, 0:LINES]
     cos_w, sin_w = tab_v[32:48, :], tab_v[48:64, :]
     row16 = iota((16, SUB), 0)
     for t in range(LINES):

time: 40.9 us -> 40.9 us (level)
  no operation moved by 1% of the time
where the time goes in v7:
time: 40.9 us; the launch traced here: 40.8 us
  Pallas kernels  40.1 us (98%)
  between operations  0.64 us (2%)
    pallas_call x1, Pallas kernels, local(): pl.pallas_call(kernel, out_shape=shapes, in_specs=[hbm] * 10, out_specs=(...  38.6 us
    pallas_call x1, Pallas kernels, local(): pl.pallas_call(write, out_shape=shapes, in_specs=[pl.BlockSpec(memory_spa...  1.55 us

profile of v7, /device:TPU:1, one launch (start us, length us, event | category | flops | bytes accessed | tf_op | source)
XLA Modules:
  0.0 40.8 jit_solution(14935724609930946551)
XLA Ops:
  0.6 38.6 %shard_map.137 = (f32[8,8,512]{2,1,0:T(8,128)S(1)}, f32[1,1]{1,0:T(1,128)}, f32[64,2048]{1,0:T(8,128)S(1)}, f32[64,68]{1,0:T(8,128)S(1)}, f32[4,64]{1,0:T(4,128)S(1)}) custom-call(f32[8,8,512]{2,1,0:T(8,128)} %vel.1, f32[8,8,512]{2,1,0:T(8,128)} %rate.1, f32[8,8,512]{2,1,0:T(8,128)} %forc.1, s32[16]{0:T(128)} %aline_h.1, s32[16]{0:T(128)} %az_h.1, ...), custom_call_target="tpu_custom_call" | custom-call | tf_op jit(solution)/shard_map/pallas_call | solution.py:467
  39.2 1.5 %shard_map.138 = (f32[8,8,512]{2,1,0:T(8,128)}, f32[1,1]{1,0:T(1,128)}, f32[64,2048]{1,0:T(8,128)}, f32[64,68]{1,0:T(8,128)}, f32[4,64]{1,0:T(4,128)}) custom-call(f32[8,8,512]{2,1,0:T(8,128)S(1)} %get-tuple-element.15.refs_0_, f32[1,1]{1,0:T(1,128)} %get-tuple-element.16.refs_1_, f32[64,2048]{1,0:T(8,128)S(1)} %get-tuple-element.17.refs_2_, ...), custom_call_target="tpu_custom_call" | custom-call | tf_op jit(solution)/shard_map/pallas_call | solution.py:509
